TPU v7x, 128 devices: a whole 4x4x4 slice. The times are simulated.
128 devices in a mesh: rows: 8 (over y, core), cols: 16 (over x, z).
Axes of the slice: x: 4, y: 4, z: 4, core: 2. Of those that a mesh axis runs over, the one named last changes fastest.
Arguments:
- lab_factors: bfloat16 [262144, 256], P(('rows', 'cols')), may hold values from -0.75 to 0.75
- patient_factors: bfloat16 [8192, 256], P('rows'), may hold values from -1.796875 to 1.796875
- values: bfloat16 [8, 1024, 128, 128], P('rows', 'cols'), may hold values from -6 to 6
- weights: bfloat16 [8, 1024, 128, 128], P('rows', 'cols'), may hold values from 0 to 5
- tile_patient: int32 [8, 1024], P('rows', 'cols'), may hold values from 0 to 7, as said below
- tile_lab: int32 [8, 1024], P('rows', 'cols'), may hold values from 0 to 127
- tile_count: int32 [8, 16], P('rows', 'cols'), may hold values from 1 to 64, as said below
- ecg_embed: bfloat16 [8192, 256], P('rows'), may hold values from -6 to 6
- ecg_map: bfloat16 [256, 256], replicated, may hold values from -0.8984375 to 0.8984375
Outputs:
- new_patient: float32 [8192, 256], P(('rows', 'cols'))
- new_lab: float32 [16, 16384, 256], P('cols', 'rows')
Inputs may be any that keep to these rules, and one draw needn't show every extreme that they name: The 64 slots of one device name distinct pairs of tile_patient and tile_lab. The slots of a device from its tile_count on are padding; some device has 64 in every draw.
All inputs are finite; a program needn't handle non-finite values.
Results may differ from a plain program's by a relative error of at most 0.0033.
Values may be sent and summed in bfloat16 or wider, within the bound.
No kernel may reach another device: no remote copies, remote signals or barrier semaphores. Data moves between devices by JAX's collectives and lax.ppermute only.
A program may use at most 128 MiB of HBM per device.

v0:
```python
import math

import jax
import jax.numpy as jnp
from jax import lax
from jax.sharding import PartitionSpec as P

ITERS = 3


ridge_term = 1.0
highest = lax.Precision.HIGHEST


def shards(
    lab_factors,
    patient_factors,
    values,
    weights,
    tile_patient,
    tile_lab,
    tile_count,
    ecg_embed,
    ecg_map,
):
    row_count = lax.axis_size("rows")
    col_count = lax.axis_size("cols")
    devices_all = row_count * col_count
    tile_size = values.shape[2]
    slot_count = values.shape[1]
    rank_size = lab_factors.shape[1]
    owned_tiles = lab_factors.shape[0] // tile_size
    per_col = owned_tiles // col_count
    col_tiles = owned_tiles * row_count
    patient_rows = patient_factors.shape[0]
    patient_tiles = patient_rows // tile_size
    own_split = lab_factors.reshape(per_col, col_count, tile_size, rank_size)
    outgoing = jnp.broadcast_to(
        own_split[:, None], (per_col, row_count, col_count, tile_size, rank_size)
    )
    outgoing = outgoing.reshape(per_col, devices_all, tile_size, rank_size)
    fetched = lax.all_to_all(outgoing, ("rows", "cols"), split_axis=1, concat_axis=1, tiled=True)
    lab_stack = fetched.reshape(per_col * devices_all, tile_size, rank_size)
    slot_lab = tile_lab[0]
    slot_patient = tile_patient[0]
    live_count = tile_count[0, 0]
    slot_pos = slot_lab % per_col * devices_all + slot_lab // per_col
    block_size = math.gcd(slot_count, 16)
    trip_count = slot_count // block_size

    def slot_block(start):
        offsets = start + jnp.arange(block_size, dtype=jnp.int32)
        live_mask = (offsets < live_count).astype(jnp.float32)
        block_weights = (
            lax.dynamic_slice_in_dim(weights[0], start, block_size).astype(jnp.float32)
            * live_mask[:, None, None]
        )
        block_values = lax.dynamic_slice_in_dim(values[0], start, block_size)
        block_patient = lax.dynamic_slice_in_dim(slot_patient, start, block_size)
        block_lab = lax.dynamic_slice_in_dim(slot_lab, start, block_size)
        lab_blocks = lab_stack[lax.dynamic_slice_in_dim(slot_pos, start, block_size)]
        return (block_weights, block_values, block_patient, block_lab, lab_blocks)

    def patient_pass(probe_tiles, with_values):

        def visit_block(block_index, running):
            block_weights, block_values, block_patient, block_lab, lab_blocks = slot_block(
                block_index * block_size
            )
            patient_blocks = probe_tiles[block_patient]
            scores = jnp.einsum(
                "tpr,tlr->tpl", patient_blocks, lab_blocks, preferred_element_type=jnp.float32
            )
            if with_values:
                kernel = block_weights * (block_values.astype(jnp.float32) - scores)
            else:
                kernel = block_weights * scores
            contrib = jnp.einsum(
                "tpl,tlr->tpr",
                kernel.astype(jnp.bfloat16),
                lab_blocks,
                preferred_element_type=jnp.float32,
            )
            return running.at[block_patient].add(contrib)

        zero_tiles = jnp.zeros((patient_tiles, tile_size, rank_size), jnp.float32)
        return lax.fori_loop(0, trip_count, visit_block, zero_tiles).reshape(
            patient_rows, rank_size
        )

    embed_map = ecg_map.astype(jnp.float32)
    share_rows = patient_rows // col_count
    share_start = lax.axis_index("cols") * share_rows
    start_guess = patient_factors.astype(jnp.float32)
    start_terms = patient_pass(patient_factors.reshape(patient_tiles, tile_size, rank_size), True)

    def reduce_terms(contrib):
        return lax.psum(contrib, "cols")

    solution = start_guess
    residual = reduce_terms(start_terms)
    residual = residual + jnp.dot(
        ecg_embed.astype(jnp.float32) - jnp.dot(solution, embed_map.T, precision=highest),
        embed_map,
        precision=highest,
    )
    residual = residual - ridge_term * solution
    direction = residual
    norm_now = jnp.sum(residual * residual, axis=1, keepdims=True)
    for iteration in range(ITERS):
        probe_tiles = direction.astype(jnp.bfloat16).reshape(patient_tiles, tile_size, rank_size)
        inner_rows = jnp.dot(direction, embed_map.T, precision=highest)
        applied = (
            reduce_terms(patient_pass(probe_tiles, False))
            + jnp.dot(inner_rows, embed_map, precision=highest)
            + ridge_term * direction
        )
        step_size = norm_now / jnp.sum(direction * applied, axis=1, keepdims=True)
        solution = solution + step_size * direction
        residual = residual - step_size * applied
        norm_next = jnp.sum(residual * residual, axis=1, keepdims=True)
        direction = residual + norm_next / norm_now * direction
        norm_now = norm_next
    patient_out = lax.dynamic_slice_in_dim(solution, share_start, share_rows)
    factor_tiles = solution.astype(jnp.bfloat16).reshape(patient_tiles, tile_size, rank_size)

    def lab_visit(block_index, running):
        block_weights, block_values, block_patient, block_lab, lab_blocks = slot_block(
            block_index * block_size
        )
        patient_blocks = factor_tiles[block_patient]
        scores = jnp.einsum(
            "tpr,tlr->tpl", patient_blocks, lab_blocks, preferred_element_type=jnp.float32
        )
        kernel = (block_weights * (block_values.astype(jnp.float32) - scores)).astype(jnp.bfloat16)
        contrib = jnp.einsum(
            "tpl,tpr->tlr", kernel, patient_blocks, preferred_element_type=jnp.float32
        )
        return running.at[block_lab].add(contrib)

    lab_partial = lax.fori_loop(
        0, trip_count, lab_visit, jnp.zeros((col_tiles, tile_size, rank_size), jnp.float32)
    )
    summed = lax.psum_scatter(lab_partial, "rows", scatter_dimension=0, tiled=True)
    my_tiles = lax.axis_index("rows") * owned_tiles + jnp.arange(owned_tiles, dtype=jnp.int32)
    own_pos = my_tiles % per_col * devices_all + my_tiles // per_col
    own_now = lab_stack[own_pos].astype(jnp.float32)
    lab_residual = summed - ridge_term * own_now
    lab_probe = lax.all_gather(lab_residual.astype(jnp.bfloat16), "rows", axis=0, tiled=True)

    def curv_visit(block_index, running):
        block_weights, block_values, block_patient, block_lab, lab_blocks = slot_block(
            block_index * block_size
        )
        inner_scores = jnp.einsum(
            "tpr,tlr->tpl",
            factor_tiles[block_patient],
            lab_probe[block_lab],
            preferred_element_type=jnp.float32,
        )
        return running.at[block_lab].add(
            jnp.sum(block_weights * inner_scores * inner_scores, axis=1)
        )

    curv_terms = lax.fori_loop(
        0, trip_count, curv_visit, jnp.zeros((col_tiles, tile_size), jnp.float32)
    )
    curvature = lax.psum_scatter(curv_terms, "rows", scatter_dimension=0, tiled=True)
    norm_lab = jnp.sum(lab_residual * lab_residual, axis=-1)
    updated = own_now + (norm_lab / (curvature + ridge_term * norm_lab))[..., None] * lab_residual
    return (patient_out, updated.reshape(1, owned_tiles * tile_size, rank_size))


def solution(mesh):
    in_specs = (
        P(("rows", "cols"), None),
        P("rows", None),
        P("rows", "cols", None, None),
        P("rows", "cols", None, None),
        P("rows", "cols"),
        P("rows", "cols"),
        P("rows", "cols"),
        P("rows", None),
        P(),
    )
    out_specs = (P(("rows", "cols"), None), P("cols", "rows", None))
    return jax.shard_map(shards, mesh=mesh, in_specs=in_specs, out_specs=out_specs, check_vma=False)
```

profile of v0, /device:TPU:1, one launch (start us, length us, event | category | flops | bytes accessed | tf_op | source)
XLA Modules:
  0.0 1000.1 jit_solution(2225692220371837361)
XLA Ops:
  7.2 5.5 broadcast_in_dim.139
  12.7 12.0 %all-to-all-start = ((bf16[1,128,128,256]{3,2,0,1:T(8,128)(2,1)}), bf16[1,128,128,256]{3,2,0,1:T(8,128)(2,1)}, u32[]{:S(2)}, u32[]{:S(2)}) async-start(bf16[1,128,128,256]{3,2,0,1:T(8,128)(2,1)} %bitcast.158), calls=%async_computation | async-start | bytes 16777216 | tf_op jit(solution)/shard_map/all_to_all | solution.py:42
  24.7 101.2 %all-to-all-done = bf16[1,128,128,256]{3,2,0,1:T(8,128)(2,1)} async-done(((bf16[1,128,128,256]{3,2,0,1:T(8,128)(2,1)}), bf16[1,128,128,256]{3,2,0,1:T(8,128)(2,1)}, u32[]{:S(2)}, u32[]{:S(2)}) %all-to-all-start) | async-done | bytes 8388640 | tf_op jit(solution)/shard_map/all_to_all | solution.py:42
  127.0 51.8 %while.79 = (s32[]{:T(128)}, f32[8,128,256]{2,1,0:T(8,128)}, s32[64]{0:T(128)S(1)}, bf16[1,64,128,128]{3,2,1,0:T(8,128)(2,1)}, s32[]{:T(128)}, /*index=5*/bf16[1...) while((s32[]{:T(128)}, f32[8,128,256]{2,1,0:T(8,128)}, ...), condition=%wide.region_2.3_spmd, body=%wide.region_0.2_spmd.sunk | while | flops 270534816 | bytes 18883936 | solution.py:87
  128.7 4.0 gather_fusion
  135.6 4.3 scatter_fusion
  141.5 4.0 gather_fusion
  148.4 4.5 scatter_fusion
  154.6 4.0 gather_fusion
  161.5 4.3 scatter_fusion
  167.5 4.0 gather_fusion
  174.4 4.3 scatter_fusion
  180.2 86.2 %all-reduce.5.cloned.1.call-done = f32[1024,256]{1,0:T(8,128)} async-done(((f32[1024,256]{1,0:T(8,128)}), f32[1024,256]{1,0:T(8,128)}) %all-reduce.5.cloned.1.call-update) | async-done | bytes 1048592 | tf_op jit(solution)/shard_map/psum | solution.py:98
  270.3 51.2 %while.80 = (s32[]{:T(128)}, f32[8,128,256]{2,1,0:T(8,128)}, s32[64]{0:T(128)S(1)}, bf16[1,64,128,128]{3,2,1,0:T(8,128)(2,1)}, s32[]{:T(128)}, /*index=5*/bf16[8...) while((s32[]{:T(128)}, f32[8,128,256]{2,1,0:T(8,128)}, ...), condition=%wide.region_7.8_spmd, body=%wide.region_5.7_spmd.sunk | while | flops 270010528 | bytes 20456812 | solution.py:87
  272.0 4.0 gather_fusion.2
  278.8 4.2 scatter_fusion.1
  284.7 4.0 gather_fusion.2
  291.4 4.5 scatter_fusion.1
  297.6 4.0 gather_fusion.2
  304.4 4.3 scatter_fusion.1
  310.4 4.0 gather_fusion.2
  317.1 4.4 scatter_fusion.1
  323.5 84.5 %all-reduce.7.cloned.1.call-done = f32[1024,256]{1,0:T(8,128)} async-done(((f32[1024,256]{1,0:T(8,128)}), f32[1024,256]{1,0:T(8,128)}) %all-reduce.7.cloned.1.call-update) | async-done | bytes 1048592 | tf_op jit(solution)/shard_map/psum | solution.py:98
  412.8 51.4 %while.81 = (s32[]{:T(128)}, f32[8,128,256]{2,1,0:T(8,128)}, s32[64]{0:T(128)S(1)}, bf16[1,64,128,128]{3,2,1,0:T(8,128)(2,1)}, s32[]{:T(128)}, /*index=5*/bf16[8...) while((s32[]{:T(128)}, f32[8,128,256]{2,1,0:T(8,128)}, ...), condition=%wide.region_13.14_spmd, body=%wide.region_11.13_spmd.sunk | while | flops 270010528 | bytes 20456812 | solution.py:87
  414.5 4.0 gather_fusion.4
  421.3 4.4 scatter_fusion.2
  427.4 4.0 gather_fusion.4
  434.2 4.4 scatter_fusion.2
  440.2 4.0 gather_fusion.4
  447.0 4.4 scatter_fusion.2
  453.1 4.0 gather_fusion.4
  459.9 4.4 scatter_fusion.2
  467.4 83.2 %all-reduce.9.cloned.1.call-done = f32[1024,256]{1,0:T(8,128)} async-done(((f32[1024,256]{1,0:T(8,128)}), f32[1024,256]{1,0:T(8,128)}) %all-reduce.9.cloned.1.call-update) | async-done | bytes 1048592 | tf_op jit(solution)/shard_map/psum | solution.py:98
  555.8 51.5 %while.82 = (s32[]{:T(128)}, f32[8,128,256]{2,1,0:T(8,128)}, s32[64]{0:T(128)S(1)}, bf16[1,64,128,128]{3,2,1,0:T(8,128)(2,1)}, s32[]{:T(128)}, /*index=5*/bf16[8...) while((s32[]{:T(128)}, f32[8,128,256]{2,1,0:T(8,128)}, ...), condition=%wide.region_19.20_spmd, body=%wide.region_17.19_spmd.sunk | while | flops 270010528 | bytes 20456812 | solution.py:87
  557.5 4.0 gather_fusion.6
  564.3 4.4 scatter_fusion.3
  570.4 4.0 gather_fusion.6
  577.2 4.4 scatter_fusion.3
  583.2 4.0 gather_fusion.6
  590.0 4.4 scatter_fusion.3
  596.1 4.0 gather_fusion.6
  602.9 4.4 scatter_fusion.3
  610.2 83.5 %all-reduce.11.cloned.1.call-done = f32[1024,256]{1,0:T(8,128)} async-done(((f32[1024,256]{1,0:T(8,128)}), f32[1024,256]{1,0:T(8,128)}) %all-reduce.11.cloned.1.call-update) | async-done | bytes 1048592 | tf_op jit(solution)/shard_map/psum | solution.py:98
  699.0 7.8 broadcast_in_dim.141
  706.8 78.3 %while.83 = (s32[]{:T(128)}, f32[128,128,256]{2,1,0:T(8,128)}, s32[64]{0:T(128)S(1)}, bf16[1,64,128,128]{3,2,1,0:T(8,128)(2,1)}, s32[]{:T(128)}, /*index=5*/bf16...) while((s32[]{:T(128)}, f32[128,128,256]{2,1,0:T(8,128)}, ...), condition=%wide.region_24.25_spmd, body=%wide.region_22.24_spmd.sunk | while | flops 270534816 | bytes 19932028 | solution.py:141
  706.9 4.0 gather_fusion.9
  721.0 5.3 scatter_fusion.4
  726.4 4.0 gather_fusion.9
  737.5 3.1 fusion.127
  740.5 5.3 scatter_fusion.4
  745.9 4.0 gather_fusion.9
  760.1 5.4 scatter_fusion.4
  765.6 4.0 gather_fusion.9
  779.7 5.4 scatter_fusion.4
  785.2 4.0 gather_fusion.12
  789.2 87.8 %reduce-scatter.3.cloned.1.call-done = f32[16,128,256]{2,1,0:T(8,128)} async-done(((f32[128,128,256]{2,1,0:T(8,128)}), f32[16,128,256]{2,1,0:T(8,128)}) %reduce-scatter.3.cloned.1.call-update) | async-done | bytes 2097168 | tf_op jit(solution)/shard_map/reduce_scatter | solution.py:144
  880.0 50.4 %all-gather.2.cloned.1.call-done = bf16[128,128,256]{2,1,0:T(8,128)(2,1)} async-done(((bf16[16,128,256]{2,1,0:T(8,128)(2,1)}), bf16[128,128,256]{2,1,0:T(8,128)(2,1)}) %all-gather.2.cloned.1.call-update) | async-done | bytes 8388624 | tf_op jit(solution)/shard_map/all_gather | solution.py:149
  930.4 30.5 %while.84 = (s32[]{:T(128)}, f32[128,128]{1,0:T(8,128)S(1)}, s32[64]{0:T(128)S(1)}, bf16[1,64,128,128]{3,2,1,0:T(8,128)(2,1)}, s32[]{:T(128)}, /*index=5*/s32[64...) while((s32[]{:T(128)}, f32[128,128]{1,0:T(8,128)S(1)}, ...), condition=%wide.region_30.31_spmd, body=%wide.region_27.30_spmd.sunk | while | flops 135530640 | bytes 6857587 | solution.py:165
  930.5 4.0 gather_fusion.11
  938.1 4.0 gather_fusion.11
  945.7 4.0 gather_fusion.11
  953.4 4.0 gather_fusion.11
  963.0 25.9 %reduce-scatter.5.cloned.1.call-done = f32[16,128]{1,0:T(8,128)} async-done(((f32[128,128]{1,0:T(8,128)}), f32[16,128]{1,0:T(8,128)}) %reduce-scatter.5.cloned.1.call-update) | async-done | bytes 8208 | tf_op jit(solution)/shard_map/reduce_scatter | solution.py:168
  989.7 3.6 convert_add_fusion
  (283 shorter events, 158.8 us)
Async XLA Ops:
  7.2 171.7 %copy-start = (bf16[256,256]{1,0:T(8,128)(2,1)S(1)}, bf16[256,256]{1,0:T(8,128)(2,1)}, u32[]{:S(2)}) copy-start(bf16[256,256]{1,0:T(8,128)(2,1)} %param.29) | copy-start | bytes 393220
  12.7 114.3 %copy-start.1 = (bf16[1024,256]{1,0:T(8,128)(2,1)S(1)}, bf16[1024,256]{1,0:T(8,128)(2,1)}, u32[]{:S(2)}) copy-start(bf16[1024,256]{1,0:T(8,128)(2,1)} %param.22) | copy-start | bytes 1572868
  12.7 114.3 %copy-start.18 = (s32[1,64]{1,0:T(1,128)S(1)}, s32[1,64]{1,0:T(1,128)}, u32[]{:S(2)}) copy-start(s32[1,64]{1,0:T(1,128)} %param.25) | copy-start | bytes 772
  12.7 114.3 %copy-start.19 = (s32[1,64]{1,0:T(1,128)S(1)}, s32[1,64]{1,0:T(1,128)}, u32[]{:S(2)}) copy-start(s32[1,64]{1,0:T(1,128)} %param.26) | copy-start | bytes 772
  12.7 113.2 %all-to-all-start = ((bf16[1,128,128,256]{3,2,0,1:T(8,128)(2,1)}), bf16[1,128,128,256]{3,2,0,1:T(8,128)(2,1)}, u32[]{:S(2)}, u32[]{:S(2)}) async-start(bf16[1,128,128,256]{3,2,0,1:T(8,128)(2,1)} %bitcast.158), calls=%async_computation | async-start | bytes 16777216 | tf_op jit(solution)/shard_map/all_to_all | solution.py:42
  24.7 241.7 %all-reduce.5.cloned.1.call-start = ((), (), s32[]{:S(2)}) async-start(), calls=%async_computation.3 | async-start | bytes 2097152 | tf_op jit(solution)/shard_map/psum | solution.py:98
  135.6 4.3 copy-start.2
  148.4 4.5 copy-start.2
  161.5 4.3 copy-start.2
  174.4 4.3 copy-start.2
  178.8 229.2 %all-reduce.7.cloned.1.call-start = ((), (), s32[]{:S(2)}) async-start(), calls=%async_computation.4 | async-start | bytes 2097152 | tf_op jit(solution)/shard_map/psum | solution.py:98
  270.3 1.7 copy-start.6
  278.7 4.2 copy-start.7
  283.0 1.7 copy-start.6
  291.4 4.5 copy-start.7
  296.0 1.7 copy-start.6
  304.4 4.3 copy-start.7
  308.7 1.7 copy-start.6
  317.1 4.4 copy-start.7
  321.5 86.5 %copy-start.10 = (f32[1024,256]{1,0:T(8,128)S(1)}, f32[1024,256]{1,0:T(8,128)}, u32[]{:S(2)}) copy-start(f32[1024,256]{1,0:T(8,128)} %get-tuple-element.1051) | copy-start | bytes 3145732
  321.5 229.1 %all-reduce.9.cloned.1.call-start = ((), (), s32[]{:S(2)}) async-start(), calls=%async_computation.5 | async-start | bytes 2097152 | tf_op jit(solution)/shard_map/psum | solution.py:98
  410.4 2.4 copy-start.14
  412.8 1.7 copy-start.8
  421.3 4.5 copy-start.9
  425.7 1.7 copy-start.8
  434.2 4.4 copy-start.9
  438.5 1.7 copy-start.8
  447.0 4.4 copy-start.9
  451.4 1.7 copy-start.8
  459.9 4.4 copy-start.9
  464.2 86.4 %copy-start.12 = (f32[1024,256]{1,0:T(8,128)S(1)}, f32[1024,256]{1,0:T(8,128)}, u32[]{:S(2)}) copy-start(f32[1024,256]{1,0:T(8,128)} %get-tuple-element.1031) | copy-start | bytes 3145732
  464.3 229.4 %all-reduce.11.cloned.1.call-start = ((), (), s32[]{:S(2)}) async-start(), calls=%async_computation.6 | async-start | bytes 2097152 | tf_op jit(solution)/shard_map/psum | solution.py:98
  467.4 85.5 %copy-start.15 = (f32[1024,256]{1,0:T(8,128)S(1)}, f32[1024,256]{1,0:T(8,128)}, u32[]{:S(2)}) copy-start(f32[1024,256]{1,0:T(8,128)} %copy-done.14) | copy-start | bytes 3145732
  555.8 1.7 copy-start.4
  564.3 4.5 copy-start.5
  568.7 1.7 copy-start.4
  577.2 4.4 copy-start.5
  581.5 1.7 copy-start.4
  590.0 4.4 copy-start.5
  594.4 1.7 copy-start.4
  602.9 4.4 copy-start.5
  607.3 269.7 %reduce-scatter.3.cloned.1.call-start = ((), (), s32[]{:S(2)}) async-start(), calls=%async_computation.7 | async-start | bytes 18874368 | tf_op jit(solution)/shard_map/reduce_scatter | solution.py:144
  610.2 86.1 %copy-start.3 = (bf16[1024,256]{1,0:T(8,128)(2,1)S(1)}, bf16[1024,256]{1,0:T(8,128)(2,1)}, u32[]{:S(2)}) copy-start(bf16[1024,256]{1,0:T(8,128)(2,1)} %param.22) | copy-start | bytes 1572868
  610.2 86.1 %copy-start.11 = (f32[1024,256]{1,0:T(8,128)S(1)}, f32[1024,256]{1,0:T(8,128)}, u32[]{:S(2)}) copy-start(f32[1024,256]{1,0:T(8,128)} %get-tuple-element.1051) | copy-start | bytes 3145732
  610.2 86.1 %copy-start.13 = (f32[1024,256]{1,0:T(8,128)S(1)}, f32[1024,256]{1,0:T(8,128)}, u32[]{:S(2)}) copy-start(f32[1024,256]{1,0:T(8,128)} %get-tuple-element.1031) | copy-start | bytes 3145732
  785.1 145.2 %all-gather.2.cloned.1.call-start = ((), (), s32[]{:S(2)}) async-start(), calls=%async_computation.8 | async-start | bytes 9437184 | tf_op jit(solution)/shard_map/all_gather | solution.py:149
  789.2 90.7 %copy-start.16 = (bf16[16,128,256]{2,1,0:T(8,128)(2,1)}, bf16[16,128,256]{2,1,0:T(8,128)(2,1)S(1)}, u32[]{:S(2)}) copy-start(bf16[16,128,256]{2,1,0:T(8,128)(2,1)S(1)} %gather_fusion.12) | copy-start | bytes 3145732
  879.9 109.1 %reduce-scatter.5.cloned.1.call-start = ((), (), s32[]{:S(2)}) async-start(), calls=%async_computation.9 | async-start | bytes 73728 | tf_op jit(solution)/shard_map/reduce_scatter | solution.py:168
  960.9 0.6 copy-start.17
Sparse Core Ops, SparseCore 0:
  178.9 87.4 all-reduce.4
  321.6 86.2 all-reduce.6
  464.4 86.1 all-reduce.8
  607.4 86.2 all-reduce.10
  785.3 91.7 reduce-scatter.2
  880.0 50.2 all-gather.1
  961.7 27.2 reduce-scatter.4
where the time goes:
time: 1010 us; the launch traced here: 1000 us
  waiting for transfers between devices  603 us (60%)
  local copies, waits for them, and re-layouts  173 us (17%)
  other arithmetic  126 us (12%)
  matrix products  70.9 us (7%)
  between operations  14.3 us (1%)
  starting transfers between devices  12.4 us (1%)
    psum x4, waiting for transfers between devices, reduce_terms(): return lax.psum(contrib, 'cols')  337 us
    all_to_all x1, waiting for transfers between devices, shards(): lax.all_to_all(outgoing, ('rows', 'cols'), split_axis=1, concat_axis=1, t...  101 us
    reduce_scatter x1, waiting for transfers between devices, shards(): lax.psum_scatter(lab_partial, 'rows', scatter_dimension=0, tiled=True)  87.8 us
    gather x20, local copies, waits for them, and re-layouts, slot_block(): lab_stack[lax.dynamic_slice_in_dim(slot_pos, start, block_size)]  79.9 us
    scatter-add x16, other arithmetic, visit_block(): return running.at[block_patient].add(contrib)  70 us
    all_gather x1, waiting for transfers between devices, shards(): lax.all_gather(lab_residual.astype(jnp.bfloat16), 'rows', axis=0, tiled=T...  50.4 us
    dot_general x16, matrix products, visit_block(): jnp.einsum('tpl,tlr->tpr', kernel.astype(jnp.bfloat16), lab_blocks, prefe...  34 us
    reduce_scatter x1, waiting for transfers between devices, shards(): lax.psum_scatter(curv_terms, 'rows', scatter_dimension=0, tiled=True)  25.9 us
  transfers between devices with their start and end apart: 8, of which 8 were waited for; matrix products, arithmetic and copies ran while one was open for 1% of the time, Pallas kernels for 0%

commit v1 on v0

v1 whole, which is shorter than its diff:
```python
import functools

import jax
import jax.numpy as jnp
from jax import lax
from jax.experimental import pallas as pl
from jax.experimental.pallas import tpu as pltpu
from jax.sharding import PartitionSpec as P

ITERS = 3
ridge_term = 1.0
highest = lax.Precision.HIGHEST
bf16 = jnp.bfloat16
f32 = jnp.float32
MIB = 1 << 20

VMEM = pl.BlockSpec(memory_space=pltpu.VMEM)
SMEM = pl.BlockSpec(memory_space=pltpu.SMEM)
ANY = pl.BlockSpec(memory_space=pl.ANY)

GROUP = 8
PASS_TYPES = (f32, bf16, bf16, bf16)


def dot_nt(a, b):
    return lax.dot_general(a, b, (((1,), (1,)), ((), ())), preferred_element_type=f32)


def dot_nn(a, b):
    return lax.dot_general(a, b, (((1,), (0,)), ((), ())), preferred_element_type=f32)


def prep_kernel(
    tiles, slots, row_ref, patient_ref, lab_ref, count_ref, x_ref, w_ref, meta_ref, xs_ref, ws_ref, *rest
):
    pieces, tmp, order, fill = rest[:-3], rest[-3], rest[-2], rest[-1]
    n = len(pieces)
    share = x_ref.shape[2] // n
    live = count_ref[0, 0]
    row = row_ref[0]

    def clear(i, carry):
        meta_ref[0, i] = 0
        return carry

    lax.fori_loop(0, meta_ref.shape[1], clear, 0)
    for p in range(tiles + 2):
        fill[p] = 0

    def key_of(s):
        return jnp.where(s < live, patient_ref[0, s], tiles)

    def count(s, carry):
        key = key_of(s)
        fill[key + 1] = fill[key + 1] + 1
        return carry

    lax.fori_loop(0, slots, count, 0)
    for p in range(tiles + 1):
        fill[p + 1] = fill[p + 1] + fill[p]
        meta_ref[0, slots + p] = fill[p]

    def place(s, carry):
        key = key_of(s)
        at = fill[key]
        fill[key] = at + 1
        order[at] = s
        meta_ref[0, at] = lab_ref[0, s]
        return carry

    lax.fori_loop(0, slots, place, 0)

    size = x_ref.shape[1]
    eye = (
        lax.broadcasted_iota(jnp.int32, (size, size), 0)
        == lax.broadcasted_iota(jnp.int32, (size, size), 1)
    ).astype(f32).astype(bf16)

    def turn(i, carry):
        for u in range(2):
            s = i * 2 + u
            src = order[s]
            vals, wts = x_ref[src], w_ref[src]
            xs_ref[s] = vals
            ws_ref[s] = wts
            tmp[u, 0] = dot_nt(eye, vals).astype(bf16)
            tmp[u, 1] = dot_nt(eye, wts).astype(bf16)
        for u in range(2):
            s = i * 2 + u
            for k in range(n):
                at = pl.multiple_of((row ^ k) * share, share)
                pieces[k][0, s] = tmp[u, 0, pl.ds(at, share), :]
                pieces[k][1, s] = tmp[u, 1, pl.ds(at, share), :]
        return carry

    lax.fori_loop(0, slots // 2, turn, 0)


def patient_chunk(with_values, first, end, x_ref, w_ref, v_ref, patients):
    at = [jnp.maximum(jnp.minimum(first + j, end - 1), 0) for j in range(GROUP)]
    labs = jnp.concatenate([v_ref[a] for a in at], axis=0)
    wts = jnp.concatenate(
        [w_ref[at[j]].astype(f32) * (first + j < end).astype(f32) for j in range(GROUP)], axis=1
    )
    scores = dot_nt(patients, labs)
    if with_values:
        vals = jnp.concatenate([x_ref[a].astype(f32) for a in at], axis=1)
        kern = wts * (vals - scores)
    else:
        kern = wts * scores
    return dot_nn(kern.astype(bf16), labs)


def patient_sums(with_values, slots, meta_ref, x_ref, w_ref, v_ref, y_ref, out_ref, acc, arrive):
    tiles = y_ref.shape[0]
    span = 2
    for p0 in range(0, tiles, span):
        group = range(p0, p0 + span)
        bounds = [(meta_ref[0, slots + p], meta_ref[0, slots + p + 1]) for p in group]
        arrive(bounds[0][0], bounds[-1][1])
        sums = [
            patient_chunk(with_values, lo, hi, x_ref, w_ref, v_ref, y_ref[p])
            for p, (lo, hi) in zip(group, bounds)
        ]
        for j in range(span):
            acc[j] = sums[j]
        for j, (p, (lo, hi)) in enumerate(zip(group, bounds)):

            def more(i, carry, j=j, p=p, lo=lo, hi=hi):
                acc[j] += patient_chunk(
                    with_values, lo + i * GROUP, hi, x_ref, w_ref, v_ref, y_ref[p]
                )
                return carry

            lax.fori_loop(1, (hi - lo + GROUP - 1) // GROUP, more, 0)
            out_ref[p] = acc[j].astype(out_ref.dtype)


def first_pass_kernel(
    slots, meta_ref, xs_any, ws_any, lab_any, y_ref, out_ref, v_ref, x_ref, w_ref, acc, v_sem, x_sem, w_sem
):
    tiles = y_ref.shape[0]
    live = meta_ref[0, slots + tiles]
    batches = (live + GROUP - 1) // GROUP

    def v_copy(s):
        return pltpu.make_async_copy(lab_any.at[meta_ref[0, s]], v_ref.at[s], v_sem.at[s])

    def batch_copies(c):
        at = pl.ds(c * GROUP, GROUP)
        return (
            pltpu.make_async_copy(xs_any.at[at], x_ref.at[at], x_sem.at[c]),
            pltpu.make_async_copy(ws_any.at[at], w_ref.at[at], w_sem.at[c]),
        )

    def start_batch(c, carry):
        for copy in batch_copies(c):
            copy.start()

        def start_slot(s, carry):
            v_copy(s).start()
            return carry

        return lax.fori_loop(c * GROUP, jnp.minimum((c + 1) * GROUP, live), start_slot, carry)

    lax.fori_loop(0, batches, start_batch, 0)

    def wait_slot(s, carry):
        v_copy(s).wait()
        return carry

    def wait_batch(c, carry):
        for copy in batch_copies(c):
            copy.wait()
        return carry

    wait_batch(0, 0)
    wait_slot(0, 0)

    def arrive(lo, hi):
        lax.fori_loop(jnp.maximum(lo, 1), hi, wait_slot, 0)
        lax.fori_loop(
            jnp.maximum((lo + GROUP - 1) // GROUP, 1), (hi + GROUP - 1) // GROUP, wait_batch, 0
        )

    patient_sums(True, slots, meta_ref, x_ref, w_ref, v_ref, y_ref, out_ref, acc, arrive)


def pass_kernel(slots, meta_ref, w_ref, v_ref, y_ref, out_ref, acc):
    patient_sums(
        False, slots, meta_ref, None, w_ref, v_ref, y_ref, out_ref, acc, lambda lo, hi: None
    )


def spread(probe_ref, rows):
    for k in range(probe_ref.shape[0]):
        probe_ref[k] = rows


def first_kernel(recv_ref, start_ref, side_ref, gram_ref, state_ref, probe_ref):
    residual = jnp.sum(recv_ref[...].astype(f32), axis=0) + side_ref[...]
    state_ref[0] = start_ref[...].astype(f32)
    state_ref[1] = residual
    state_ref[2] = residual
    state_ref[3] = (
        jnp.dot(residual, gram_ref[...], precision=highest, preferred_element_type=f32)
        + ridge_term * residual
    )
    spread(probe_ref, residual.astype(bf16))


def step_kernel(last, recv_ref, state_in, gram_ref, state_ref, probe_ref):
    residual = state_in[1]
    direction = state_in[2]
    applied = jnp.sum(recv_ref[...].astype(f32), axis=0) + state_in[3]
    norm_now = jnp.sum(residual * residual, axis=1, keepdims=True)
    step_size = norm_now / jnp.sum(direction * applied, axis=1, keepdims=True)
    solution_now = state_in[0] + step_size * direction
    if last:
        state_ref[...] = solution_now
        spread(probe_ref, solution_now.astype(bf16))
        return
    residual = residual - step_size * applied
    norm_next = jnp.sum(residual * residual, axis=1, keepdims=True)
    direction = residual + norm_next / norm_now * direction
    state_ref[0] = solution_now
    state_ref[1] = residual
    state_ref[2] = direction
    state_ref[3] = (
        jnp.dot(direction, gram_ref[...], precision=highest, preferred_element_type=f32)
        + ridge_term * direction
    )
    spread(probe_ref, direction.astype(bf16))


def lab_kernel(slots, n, row_ref, meta_ref, *refs):
    pieces = refs[:n]
    f_own, f_two, f_six, f_top, f_low, g_own, g_two, g_six, g_top, g_low = refs[n : n + 10]
    lab_any, out_ref, xw, f_ref, v_ref, acc, probe, curv, p_sem, f_sem, v_sem = refs[n + 10 :]
    tiles = f_ref.shape[0] // n
    half = tiles // 2
    share = v_ref.shape[1]
    size = f_ref.shape[1]
    row = row_ref[0]
    v_copy = pltpu.make_async_copy(lab_any.at[:, row], v_ref, v_sem)
    v_copy.start()
    p_copies = [pltpu.make_async_copy(pieces[k], xw.at[k], p_sem.at[k]) for k in range(n)]
    whole = {0: f_own, 1: g_own, 2: f_two, 3: g_two, 6: f_six, 7: g_six}
    halves = {4: (f_top, f_low), 5: (g_top, g_low)}
    f_copies = {}
    for k, ref in whole.items():
        f_copies[k] = [
            pltpu.make_async_copy(ref, f_ref.at[pl.ds((row ^ k) * tiles, tiles)], f_sem.at[k])
        ]
    for k, pair in halves.items():
        f_copies[k] = [
            pltpu.make_async_copy(
                ref, f_ref.at[pl.ds((row ^ k) * tiles + h * half, half)], f_sem.at[n * h + k]
            )
            for h, ref in enumerate(pair)
        ]
    for k in range(n):
        p_copies[k].start()
        for copy in f_copies[k]:
            copy.start()
    acc[...] = jnp.zeros_like(acc)
    curv[...] = jnp.zeros_like(curv)
    v_copy.wait()
    for k in range(n):
        p_copies[k].wait()
        for copy in f_copies[k]:
            copy.wait()

    span = GROUP * share
    side_by_side = 4
    row_slot = lax.broadcasted_iota(jnp.int32, (span, size), 0) // share

    def take(k, source, first, end):
        base = jnp.minimum(first, slots - GROUP)
        labs = [meta_ref[source, base + j] for j in range(GROUP)]
        inside = (row_slot >= first - base) & (row_slot < end - base)
        wts = xw[k, 1, pl.ds(base, GROUP)].reshape(span, size).astype(f32)
        return base, labs, jnp.where(inside, wts, 0.0)

    def sweep(terms_of, total):
        def add(labs, terms):
            for j, t in enumerate(labs):
                total[t] += terms[j * share : (j + 1) * share]

        def of_source(k, carry):
            source = row ^ k

            def of_tiles(q, carry):
                tile = [q * side_by_side + j for j in range(side_by_side)]
                lo = [meta_ref[source, slots + p] for p in tile]
                hi = [meta_ref[source, slots + p + 1] for p in tile]
                found = [
                    terms_of(k, source, lo[j], hi[j], source * tiles + tile[j])
                    for j in range(side_by_side)
                ]
                for labs, terms in found:
                    add(labs, terms)
                for j in range(side_by_side):

                    def more(i, carry, j=j):
                        add(*terms_of(k, source, lo[j] + i * GROUP, hi[j], source * tiles + tile[j]))
                        return carry

                    lax.fori_loop(1, (hi[j] - lo[j] + GROUP - 1) // GROUP, more, 0)
                return carry

            return lax.fori_loop(0, tiles // side_by_side, of_tiles, carry)

        lax.fori_loop(0, n, of_source, 0)

    def residual_terms(k, source, first, end, at):
        base, labs, wts = take(k, source, first, end)
        rows = jnp.concatenate([v_ref[t] for t in labs], axis=0)
        vals = xw[k, 0, pl.ds(base, GROUP)].reshape(span, size).astype(f32)
        kern = (wts * (vals - dot_nt(rows, f_ref[at]))).astype(bf16)
        return labs, dot_nn(kern, f_ref[at])

    sweep(residual_terms, acc)

    block = 16

    def finish(i, carry):
        at = pl.ds(i * block, block)
        rest = acc[at] - ridge_term * v_ref[at].astype(f32)
        acc[at] = rest
        probe[at] = rest.astype(bf16)
        return carry

    lax.fori_loop(0, acc.shape[0] // block, finish, 0)

    def curvature_terms(k, source, first, end, at):
        base, labs, wts = take(k, source, first, end)
        rows = jnp.concatenate([probe[t] for t in labs], axis=0)
        inner = dot_nt(rows, f_ref[at])
        return labs, wts * inner * inner

    sweep(curvature_terms, curv)

    def emit(i, carry):
        at = pl.ds(i * block, block)
        rest = acc[at]
        norm = jnp.sum(rest * rest, axis=-1, keepdims=True)
        total = jnp.sum(curv[at], axis=-1, keepdims=True) + ridge_term * norm
        out_ref[at] = (norm / total * rest).astype(out_ref.dtype)
        return carry

    lax.fori_loop(0, acc.shape[0] // block, emit, 0)


def shape_of(shape, dtype):
    return jax.ShapeDtypeStruct(shape, dtype)


def params(mib):
    return pltpu.CompilerParams(vmem_limit_bytes=mib * MIB)


def shards(
    lab_factors,
    patient_factors,
    values,
    weights,
    tile_patient,
    tile_lab,
    tile_count,
    ecg_embed,
    ecg_map,
):
    rows = lax.axis_size("rows")
    cols = lax.axis_size("cols")
    size = values.shape[2]
    slots = values.shape[1]
    rank = lab_factors.shape[1]
    owned_tiles = lab_factors.shape[0] // size
    col_tiles = owned_tiles * rows
    patient_rows = patient_factors.shape[0]
    tiles = patient_rows // size
    share_rows = patient_rows // cols
    lab_share = size // rows
    row = lax.axis_index("rows").astype(jnp.int32).reshape(1)
    x, w = values[0], weights[0]

    own_labs = lax.all_to_all(lab_factors, "cols", split_axis=0, concat_axis=0, tiled=True)
    labs = lax.all_gather(own_labs, "rows", axis=0, tiled=True)

    slot_shape = shape_of((slots, size, size), bf16)
    out_pieces = [shape_of((2, slots, lab_share, size), bf16)] * rows
    prep = pl.pallas_call(
        functools.partial(prep_kernel, tiles, slots),
        out_shape=[shape_of((1, 128), jnp.int32), slot_shape, slot_shape] + out_pieces,
        in_specs=[SMEM] * 4 + [VMEM] * 2,
        out_specs=[SMEM] + [VMEM] * (rows + 2),
        scratch_shapes=[
            pltpu.VMEM((2, 2, size, size), bf16),
            pltpu.SMEM((slots,), jnp.int32),
            pltpu.SMEM((tiles + 2,), jnp.int32),
        ],
        compiler_params=params(28),
        name="prep",
    )(row, tile_patient, tile_lab, tile_count, x, w)
    meta, xs, ws, pieces = prep[0], prep[1], prep[2], list(prep[3:])
    meta_all = lax.all_gather(meta, "rows", axis=0, tiled=True)

    embed_map = ecg_map.astype(f32)
    gram = jnp.dot(embed_map.T, embed_map, precision=highest)
    share_at = lax.axis_index("cols") * share_rows
    start_share = lax.dynamic_slice_in_dim(patient_factors, share_at, share_rows).astype(f32)
    embed_share = lax.dynamic_slice_in_dim(ecg_embed, share_at, share_rows).astype(f32)
    side = (
        jnp.dot(
            embed_share - jnp.dot(start_share, embed_map.T, precision=highest),
            embed_map,
            precision=highest,
        )
        - ridge_term * start_share
    )

    labs, pieces, meta_all, side, gram, start_share = lax.optimization_barrier(
        (labs, pieces, meta_all, side, gram, start_share)
    )
    lab_tiles = labs.reshape(col_tiles, size, rank)

    def swap(array, k):
        return lax.ppermute(array, "rows", [(i, i ^ k) for i in range(rows)])

    def send_pieces(now, keys):
        if not keys:
            return now, lambda later: later
        held = lax.optimization_barrier((now, [pieces[k] for k in keys]))
        moved = [swap(piece, k) for piece, k in zip(held[1], keys)]

        def end(later):
            later, done = lax.optimization_barrier((later, moved))
            for k, piece in zip(keys, done):
                pieces[k] = piece
            return later

        return held[0], end

    def exchange(partial):
        partial = partial.reshape(patient_rows, rank)
        recv = lax.all_to_all(partial, "cols", split_axis=0, concat_axis=0, tiled=True)
        return recv.reshape(cols, share_rows, rank)

    def to_all(probe):
        probe = probe.reshape(patient_rows, rank)
        probe = lax.all_to_all(probe, "cols", split_axis=0, concat_axis=0, tiled=True)
        return probe.reshape(tiles, size, rank)

    state_shape = shape_of((4, share_rows, rank), f32)
    probe_shape = shape_of((cols, share_rows, rank), bf16)
    stages = ((1, 2), (3, 4), (5, 6), (7,))
    lab_tiles, end = send_pieces(lab_tiles, stages[0])
    partial, slot_labs = pl.pallas_call(
        functools.partial(first_pass_kernel, slots),
        out_shape=[
            shape_of((tiles, size, rank), PASS_TYPES[0]),
            shape_of((slots, size, rank), bf16),
        ],
        in_specs=[SMEM, ANY, ANY, ANY, VMEM],
        out_specs=[VMEM] * 2,
        scratch_shapes=[
            pltpu.VMEM((slots, size, size), bf16),
            pltpu.VMEM((slots, size, size), bf16),
            pltpu.VMEM((2, size, rank), f32),
            pltpu.SemaphoreType.DMA((slots,)),
            pltpu.SemaphoreType.DMA((slots // GROUP,)),
            pltpu.SemaphoreType.DMA((slots // GROUP,)),
        ],
        compiler_params=params(24),
        name="first_pass",
    )(meta, xs, ws, lab_tiles, patient_factors.reshape(tiles, size, rank))
    recv = end(exchange(partial))
    state, probe = pl.pallas_call(
        first_kernel,
        out_shape=[state_shape, probe_shape],
        in_specs=[VMEM] * 4,
        out_specs=[VMEM] * 2,
        compiler_params=params(8),
        name="first_step",
    )(recv, start_share, side, gram)
    for iteration in range(ITERS):
        last = iteration == ITERS - 1
        probe, end = send_pieces(probe, stages[iteration + 1])
        partial = pl.pallas_call(
            functools.partial(pass_kernel, slots),
            out_shape=shape_of((tiles, size, rank), PASS_TYPES[iteration + 1]),
            in_specs=[SMEM] + [VMEM] * 3,
            out_specs=VMEM,
            scratch_shapes=[pltpu.VMEM((2, size, rank), f32)],
            compiler_params=params(16),
            name="patient_pass",
        )(meta, ws, slot_labs, to_all(probe))
        recv = end(exchange(partial))
        state, probe = pl.pallas_call(
            functools.partial(step_kernel, last),
            out_shape=[shape_of((share_rows, rank), f32) if last else state_shape, probe_shape],
            in_specs=[VMEM] * 3,
            out_specs=[VMEM] * 2,
            compiler_params=params(8),
            name="step",
        )(recv, state, gram)
    patient_out = state

    f_own = to_all(probe)
    half = tiles // 2
    f_two, f_six = swap(f_own, 2), swap(f_own, 6)
    f_top, f_low = swap(f_six[:half], 2), swap(f_two[half:], 6)
    here = [f_own, f_two, f_six, f_top, f_low]
    factors = here + [swap(part, 1) for part in here]
    delta = pl.pallas_call(
        functools.partial(lab_kernel, slots, rows),
        out_shape=shape_of((col_tiles, lab_share, rank), bf16),
        in_specs=[SMEM] * 2 + [ANY] * (rows + len(factors) + 1),
        out_specs=VMEM,
        scratch_shapes=[
            pltpu.VMEM((rows, 2, slots, lab_share, size), bf16),
            pltpu.VMEM((rows * tiles, size, rank), bf16),
            pltpu.VMEM((col_tiles, lab_share, rank), bf16),
            pltpu.VMEM((col_tiles, lab_share, rank), f32),
            pltpu.VMEM((col_tiles, lab_share, rank), bf16),
            pltpu.VMEM((col_tiles, lab_share, size), f32),
            pltpu.SemaphoreType.DMA((rows,)),
            pltpu.SemaphoreType.DMA((2 * rows,)),
            pltpu.SemaphoreType.DMA,
        ],
        compiler_params=params(32),
        name="lab_step",
    )(row, meta_all, *pieces, *factors, lab_tiles.reshape(col_tiles, rows, lab_share, rank))
    back = lax.all_to_all(
        delta.reshape(col_tiles * lab_share, rank), "rows", split_axis=0, concat_axis=0, tiled=True
    )
    back = back.reshape(rows, owned_tiles, lab_share, rank).transpose(1, 0, 2, 3)
    updated = own_labs.reshape(owned_tiles, rows, lab_share, rank).astype(f32) + back.astype(f32)
    return (patient_out, updated.reshape(1, owned_tiles * size, rank))


def solution(mesh):
    in_specs = (
        P(("rows", "cols"), None),
        P("rows", None),
        P("rows", "cols", None, None),
        P("rows", "cols", None, None),
        P("rows", "cols"),
        P("rows", "cols"),
        P("rows", "cols"),
        P("rows", None),
        P(),
    )
    out_specs = (P(("rows", "cols"), None), P("cols", "rows", None))
    return jax.shard_map(shards, mesh=mesh, in_specs=in_specs, out_specs=out_specs, check_vma=False)
```

time: 1010 us -> 334 us (0.33)
  waiting for transfers between devices: 603 us -> 78.6 us
  local copies, waits for them, and re-layouts: 173 us -> 38.2 us
  other arithmetic: 126 us -> 2.31 us
  matrix products: 70.9 us -> 1.99 us
  blocking collectives: 0 us -> 67.2 us
  starting transfers between devices: 12.4 us -> 74 us
  Pallas kernels: 0 us -> 53.6 us
    psum x4 -> x0, waiting for transfers between devices: 337 us -> none  [reduce_terms(): return lax.psum(contrib, 'cols')]
    gather x49 -> x0, local copies, waits for them, and re-layouts: 130 us -> none  [the longest x20 79.9 us: slot_block(): lab_stack[lax.dynamic_slice_in_dim(slot_pos, start, block_size)]]
    reduce_scatter x2 -> x0, waiting for transfers between devices: 114 us -> none  [the longest x1 87.8 us: shards(): lax.psum_scatter(lab_partial, 'rows', scatter_dimension=0, tiled=True)]
    scatter-add x24 -> x0, other arithmetic: 94.3 us -> none  [the longest x16 70 us: visit_block(): return running.at[block_patient].add(contrib)]
    dot_general x32 -> x3, matrix products: 70.9 us -> 1.99 us  [the longest x1 0.91 us: shards(): jnp.dot(start_share, embed_map.T, precision=highest)]
    all_to_all x1 -> x7, waiting for transfers between devices: 101 us -> 39.1 us  [the longest x4 20 us: exchange(): lax.all_to_all(partial, 'cols', split_axis=0, concat_axis=0, tiled=True)]
    all_to_all x0 -> x3, blocking collectives: none -> 54.7 us  [the longest x1 24.5 us: shards(): lax.all_to_all(lab_factors, 'cols', split_axis=0, concat_axis=0, tiled=True)]
    pallas_call x0 -> x10, Pallas kernels: none -> 53.6 us  [the longest x1 19.8 us: shards(): pl.pallas_call(functools.partial(lab_kernel, slots, rows), out_shape=shap...]
  transfers between devices with their start and end apart: 8 -> 24, of which waited for: 8 -> 14; matrix products, arithmetic and copies ran while one was open for 1% -> 1% of each run, Pallas kernels for 0% -> 7%
where the time goes in v1:
time: 334 us; the launch traced here: 331 us
  waiting for transfers between devices  78.6 us (24%)
  starting transfers between devices  74 us (22%)
  blocking collectives  67.2 us (20%)
  Pallas kernels  53.6 us (16%)
  local copies, waits for them, and re-layouts  38.2 us (11%)
  between operations  15 us (4%)
    unnamed x78, local copies, waits for them, and re-layouts  38.1 us
    ppermute x16, starting transfers between devices, swap(): return lax.ppermute(array, 'rows', [(i, i ^ k) for i in range(rows)])  32.5 us
    all_to_all x4, starting transfers between devices, exchange(): lax.all_to_all(partial, 'cols', split_axis=0, concat_axis=0, tiled=True)  29.6 us
    ppermute x16, waiting for transfers between devices, swap(): return lax.ppermute(array, 'rows', [(i, i ^ k) for i in range(rows)])  27.1 us
    all_to_all x1, blocking collectives, shards(): lax.all_to_all(lab_factors, 'cols', split_axis=0, concat_axis=0, tiled=True)  24.5 us
    all_to_all x4, waiting for transfers between devices, exchange(): lax.all_to_all(partial, 'cols', split_axis=0, concat_axis=0, tiled=True)  20 us
    pallas_call x1, Pallas kernels, shards(): pl.pallas_call(functools.partial(lab_kernel, slots, rows), out_shape=shap...  19.8 us
    all_to_all x3, waiting for transfers between devices, to_all(): lax.all_to_all(probe, 'cols', split_axis=0, concat_axis=0, tiled=True)  19.1 us
  transfers between devices with their start and end apart: 24, of which 14 were waited for; matrix products, arithmetic and copies ran while one was open for 1% of the time, Pallas kernels for 7%

profile of v1, /device:TPU:1, one launch (start us, length us, event | category | flops | bytes accessed | tf_op | source)
XLA Modules:
  0.0 330.8 jit_solution(17847343388059821992)
XLA Ops:
  7.2 24.5 %all_to_all.81 = bf16[16,128,256]{2,1,0:T(8,128)(2,1)} all-to-all(bf16[16,128,256]{2,1,0:T(8,128)(2,1)} %bitcast.51), channel_id=1, replica_groups=mesh['rows'=8,'cols'=16] {'cols'}, dimensions={0} | all-to-all | bytes 2097152 | tf_op jit(solution)/shard_map/all_to_all | solution.py:388
  32.5 1.6 copy-done.9
  34.1 1.6 copy-done.10
  35.7 10.9 %prep.1 = (s32[1,128]{1,0:T(1,128)S(1)}, bf16[64,128,128]{2,1,0:T(8,128)(2,1)S(1)}, bf16[64,128,128]{2,1,0:T(8,128)(2,1)S(1)}, bf16[2,64,16,128]{3,2,1,0:T(8,128...) custom-call(s32[1]{0:T(128)} %bitcast.row_ref, ...), custom_call_target="tpu_custom_call" | custom-call | tf_op jit(solution)/shard_map/prep/pallas_call | solution.py:393
  46.6 1.3 copy-done.7
  49.5 0.8 copy-done.32
  54.3 12.5 %all-gather = s32[8,1,128]{2,1,0:T(1,128)S(1)} all-gather(s32[1,1,128]{2,1,0:T(1,128)S(1)} %bitcast.46), channel_id=1, replica_groups=mesh['rows'=8,'cols'=16] {'rows'}, dimensions={0}, use_global_device_ids=true | all-gather | bytes 4608 | tf_op jit(solution)/shard_map/all_gather | solution.py:407
  67.4 0.9 convolution_subtract_fusion.1
  68.3 0.9 convolution_subtract_fusion.side_ref
  69.4 12.4 %all-gather.3.cloned.1.call-done = bf16[16384,256]{1,0:T(8,128)(2,1)} async-done(((bf16[2048,256]{1,0:T(8,128)(2,1)}), bf16[16384,256]{1,0:T(8,128)(2,1)}) %all-gather.3.cloned.1.call-update) | async-done | bytes 8388624 | tf_op jit(solution)/shard_map/all_gather | solution.py:389
  81.8 3.4 %copy-done.5 = bf16[16384,256]{1,0:T(8,128)(2,1)S(1)} copy-done((bf16[16384,256]{1,0:T(8,128)(2,1)S(1)}, bf16[16384,256]{1,0:T(8,128)(2,1)}, u32[]{:S(2)}) %copy-start.5) | copy-done | bytes 8388632
  85.2 1.6 copy-done.8
  86.8 7.1 %first_pass.1 = (f32[8,128,256]{2,1,0:T(8,128)S(1)}, bf16[64,128,256]{2,1,0:T(8,128)(2,1)S(1)}) custom-call(s32[1,128]{1,0:T(1,128)S(1)} %get-tuple-element.58.meta_ref, bf16[64,128,128]{2,1,0:T(8,128)(2,1)S(1)} %copy-done.8, bf16[64,128,128]{2,1,0:T(8,128)(2,1)S(1)} %get-tuple-element.59.ws_any.w_ref, bf16[128,128,256]{2,1,0:T(8,128)(2,1)S(1)} %bitcast.31, ...), custom_call_target="tpu_custom_call" | custom-call | tf_op jit(solution)/shard_map/first_pass/pallas_call | solution.py:459
  93.9 2.1 copy-done.1
  96.0 1.0 copy-done.11
  97.0 12.6 %all-to-all-start.1 = ((f32[16,64,256]{2,1,0:T(8,128)}), f32[16,64,256]{2,1,0:T(8,128)S(1)}, u32[]{:S(2)}, u32[]{:S(2)}) async-start(f32[16,64,256]{2,1,0:T(8,128)} %bitcast.43), calls=%async_computation.1 | async-start | bytes 2097152 | tf_op jit(solution)/shard_map/all_to_all | solution.py:447
  109.8 2.0 collective-permute-done.refs_1_
  112.6 10.5 %collective-permute-done.1.refs_2_ = bf16[2,64,16,128]{3,2,1,0:T(8,128)(2,1)S(1)} collective-permute-done((bf16[2,64,16,128]{3,2,1,0:T(8,128)(2,1)}, bf16[2,64,16,128]{3,2,1,0:T(8,128)(2,1)S(1)}, u32[]{:S(2)}, u32[]{:S(2)}) %collective-permute-start.1) | collective-permute-done | bytes 524320 | tf_op jit(solution)/shard_map/ppermute | solution.py:429
  123.9 2.6 all-to-all-done.1.recv_ref
  126.4 0.8 copy-done.23
  127.3 0.8 copy-done.24
  129.9 4.0 %all-to-all-start.2 = ((bf16[16,64,256]{2,1,0:T(8,128)(2,1)}), bf16[16,64,256]{2,1,0:T(8,128)(2,1)S(1)}, u32[]{:S(2)}, u32[]{:S(2)}) async-start(bf16[16,64,256]{2,1,0:T(8,128)(2,1)} %copy-done.21), calls=%async_computation.2 | async-start | bytes 1048576 | tf_op jit(solution)/shard_map/all_to_all | solution.py:452
  134.0 1.5 collective-permute-start.2
  135.5 1.1 collective-permute-start.3
  136.6 6.3 %all-to-all-done.2 = bf16[16,64,256]{2,1,0:T(8,128)(2,1)S(1)} async-done(((bf16[16,64,256]{2,1,0:T(8,128)(2,1)}), bf16[16,64,256]{2,1,0:T(8,128)(2,1)S(1)}, u32[]{:S(2)}, u32[]{:S(2)}) %all-to-all-start.2) | async-done | bytes 524320 | tf_op jit(solution)/shard_map/all_to_all | solution.py:452
  142.9 2.2 copy-done.2
  145.1 4.5 %patient_pass.3 = bf16[8,128,256]{2,1,0:T(8,128)(2,1)} custom-call(s32[1,128]{1,0:T(1,128)S(1)} %get-tuple-element.58.meta_ref, bf16[64,128,128]{2,1,0:T(8,128)(2,1)S(1)} %get-tuple-element.59.ws_any.w_ref, bf16[64,128,256]{2,1,0:T(8,128)(2,1)S(1)} %copy-done.2, bf16[8,128,256]{2,1,0:T(8,128)(2,1)S(1)} %bitcast.40), custom_call_target="tpu_custom_call" | custom-call | tf_op jit(solution)/shard_map/patient_pass/pallas_call | solution.py:490
  149.5 6.2 %all-to-all-start.3 = ((bf16[16,64,256]{2,1,0:T(8,128)(2,1)}), bf16[16,64,256]{2,1,0:T(8,128)(2,1)S(1)}, u32[]{:S(2)}, u32[]{:S(2)}) async-start(bf16[16,64,256]{2,1,0:T(8,128)(2,1)} %bitcast.11), calls=%async_computation.3 | async-start | bytes 1048576 | tf_op jit(solution)/shard_map/all_to_all | solution.py:447
  155.8 4.5 %collective-permute-done.3.refs_4_ = bf16[2,64,16,128]{3,2,1,0:T(8,128)(2,1)} collective-permute-done((bf16[2,64,16,128]{3,2,1,0:T(8,128)(2,1)}, bf16[2,64,16,128]{3,2,1,0:T(8,128)(2,1)}, u32[]{:S(2)}, u32[]{:S(2)}) %collective-permute-start.3) | collective-permute-done | bytes 524320 | tf_op jit(solution)/shard_map/ppermute | solution.py:429
  160.3 5.8 %all-to-all-done.3.recv_ref = bf16[16,64,256]{2,1,0:T(8,128)(2,1)S(1)} async-done(((bf16[16,64,256]{2,1,0:T(8,128)(2,1)}), bf16[16,64,256]{2,1,0:T(8,128)(2,1)S(1)}, u32[]{:S(2)}, u32[]{:S(2)}) %all-to-all-start.3) | async-done | bytes 524320 | tf_op jit(solution)/shard_map/all_to_all | solution.py:447
  166.1 0.9 copy-done.26
  169.0 3.6 %all-to-all-start.4 = ((bf16[16,64,256]{2,1,0:T(8,128)(2,1)}), bf16[16,64,256]{2,1,0:T(8,128)(2,1)S(1)}, u32[]{:S(2)}, u32[]{:S(2)}) async-start(bf16[16,64,256]{2,1,0:T(8,128)(2,1)} %copy-done.22), calls=%async_computation.4 | async-start | bytes 1048576 | tf_op jit(solution)/shard_map/all_to_all | solution.py:452
  172.6 2.7 collective-permute-start.4
  175.3 1.5 collective-permute-start.5
  176.8 5.0 %all-to-all-done.4 = bf16[16,64,256]{2,1,0:T(8,128)(2,1)S(1)} async-done(((bf16[16,64,256]{2,1,0:T(8,128)(2,1)}), bf16[16,64,256]{2,1,0:T(8,128)(2,1)S(1)}, u32[]{:S(2)}, u32[]{:S(2)}) %all-to-all-start.4) | async-done | bytes 524320 | tf_op jit(solution)/shard_map/all_to_all | solution.py:452
  181.8 2.2 copy-done.3
  184.0 4.3 %patient_pass.4 = bf16[8,128,256]{2,1,0:T(8,128)(2,1)} custom-call(s32[1,128]{1,0:T(1,128)S(1)} %get-tuple-element.58.meta_ref, bf16[64,128,128]{2,1,0:T(8,128)(2,1)S(1)} %get-tuple-element.59.ws_any.w_ref, bf16[64,128,256]{2,1,0:T(8,128)(2,1)S(1)} %copy-done.3, bf16[8,128,256]{2,1,0:T(8,128)(2,1)S(1)} %bitcast.41), custom_call_target="tpu_custom_call" | custom-call | tf_op jit(solution)/shard_map/patient_pass/pallas_call | solution.py:490
  188.3 5.4 %all-to-all-start.5 = ((bf16[16,64,256]{2,1,0:T(8,128)(2,1)}), bf16[16,64,256]{2,1,0:T(8,128)(2,1)S(1)}, u32[]{:S(2)}, u32[]{:S(2)}) async-start(bf16[16,64,256]{2,1,0:T(8,128)(2,1)} %bitcast.13), calls=%async_computation.5 | async-start | bytes 1048576 | tf_op jit(solution)/shard_map/all_to_all | solution.py:447
  193.7 6.5 %collective-permute-done.5.refs_6_ = bf16[2,64,16,128]{3,2,1,0:T(8,128)(2,1)} collective-permute-done((bf16[2,64,16,128]{3,2,1,0:T(8,128)(2,1)}, bf16[2,64,16,128]{3,2,1,0:T(8,128)(2,1)}, u32[]{:S(2)}, u32[]{:S(2)}) %collective-permute-start.5) | collective-permute-done | bytes 524320 | tf_op jit(solution)/shard_map/ppermute | solution.py:429
  200.2 2.4 all-to-all-done.5.recv_ref
  202.7 0.9 copy-done.28
  203.6 1.1 step.4
  204.7 4.3 %all-to-all-start.6 = ((bf16[16,64,256]{2,1,0:T(8,128)(2,1)}), bf16[16,64,256]{2,1,0:T(8,128)(2,1)S(1)}, u32[]{:S(2)}, u32[]{:S(2)}) async-start(bf16[16,64,256]{2,1,0:T(8,128)(2,1)} %get-tuple-element.99), calls=%async_computation.6 | async-start | bytes 1048576 | tf_op jit(solution)/shard_map/all_to_all | solution.py:452
  209.0 1.3 collective-permute-start.6
  210.3 7.8 %all-to-all-done.6 = bf16[16,64,256]{2,1,0:T(8,128)(2,1)S(1)} async-done(((bf16[16,64,256]{2,1,0:T(8,128)(2,1)}), bf16[16,64,256]{2,1,0:T(8,128)(2,1)S(1)}, u32[]{:S(2)}, u32[]{:S(2)}) %all-to-all-start.6) | async-done | bytes 524320 | tf_op jit(solution)/shard_map/all_to_all | solution.py:452
  218.2 2.2 copy-done.4
  220.4 4.3 %patient_pass.5 = bf16[8,128,256]{2,1,0:T(8,128)(2,1)} custom-call(s32[1,128]{1,0:T(1,128)S(1)} %get-tuple-element.58.meta_ref, bf16[64,128,128]{2,1,0:T(8,128)(2,1)S(1)} %get-tuple-element.59.ws_any.w_ref, bf16[64,128,256]{2,1,0:T(8,128)(2,1)S(1)} %copy-done.4, bf16[8,128,256]{2,1,0:T(8,128)(2,1)S(1)} %bitcast.42), custom_call_target="tpu_custom_call" | custom-call | tf_op jit(solution)/shard_map/patient_pass/pallas_call | solution.py:490
  224.7 5.4 %all-to-all-start.7 = ((bf16[16,64,256]{2,1,0:T(8,128)(2,1)}), bf16[16,64,256]{2,1,0:T(8,128)(2,1)S(1)}, u32[]{:S(2)}, u32[]{:S(2)}) async-start(bf16[16,64,256]{2,1,0:T(8,128)(2,1)} %bitcast.15), calls=%async_computation.7 | async-start | bytes 1048576 | tf_op jit(solution)/shard_map/all_to_all | solution.py:447
  230.1 9.2 %all-to-all-done.7.recv_ref = bf16[16,64,256]{2,1,0:T(8,128)(2,1)S(1)} async-done(((bf16[16,64,256]{2,1,0:T(8,128)(2,1)}), bf16[16,64,256]{2,1,0:T(8,128)(2,1)S(1)}, u32[]{:S(2)}, u32[]{:S(2)}) %all-to-all-start.7) | async-done | bytes 524320 | tf_op jit(solution)/shard_map/all_to_all | solution.py:447
  240.1 12.1 %all_to_all.82 = bf16[16,64,256]{2,1,0:T(8,128)(2,1)S(1)} all-to-all(bf16[16,64,256]{2,1,0:T(8,128)(2,1)S(1)} %get-tuple-element.113), channel_id=1, replica_groups=mesh['rows'=8,'cols'=16] {'cols'}, dimensions={0} | all-to-all | bytes 1048576 | tf_op jit(solution)/shard_map/all_to_all | solution.py:452
  252.3 3.7 %collective-permute-start.7 = (bf16[8,128,256]{2,1,0:T(8,128)(2,1)S(1)}, bf16[8,128,256]{2,1,0:T(8,128)(2,1)S(1)}, u32[]{:S(2)}, u32[]{:S(2)}) collective-permute-start(bf16[8,128,256]{2,1,0:T(8,128)(2,1)S(1)} %bitcast.35), channel_id=1, source_target_pairs={{0,32},{16,48},{32,0},{48,16},{64,96},{80,112},{96,64},{112,80},{1... | collective-permute-start | bytes 1572872 | tf_op jit(solution)/shard_map/ppermute | solution.py:429
  256.0 4.0 %collective-permute-start.11 = (bf16[8,128,256]{2,1,0:T(8,128)(2,1)S(1)}, bf16[8,128,256]{2,1,0:T(8,128)(2,1)S(1)}, u32[]{:S(2)}, u32[]{:S(2)}) collective-permute-start(bf16[8,128,256]{2,1,0:T(8,128)(2,1)S(1)} %bitcast.36), channel_id=1, source_target_pairs={{0,16},{16,0},{32,48},{48,32},{64,80},{80,64},{96,112},{112,96},{1... | collective-permute-start | bytes 1572872 | tf_op jit(solution)/shard_map/ppermute | solution.py:429
  260.0 2.4 collective-permute-done.8.refs_10_
  262.4 2.5 collective-permute-start.9
  264.9 1.9 collective-permute-start.10
  266.8 5.9 %collective-permute-start.13 = (bf16[8,128,256]{2,1,0:T(8,128)(2,1)S(1)}, bf16[8,128,256]{2,1,0:T(8,128)(2,1)S(1)}, u32[]{:S(2)}, u32[]{:S(2)}) collective-permute-start(bf16[8,128,256]{2,1,0:T(8,128)(2,1)S(1)} %collective-permute-done.8.refs_10_), channel_id=1, source_target_pairs={{0,16},{16,0},{32,48},{48,32},{64,80},{80,64},{96,112},{112,96},{1... | collective-permute-start | bytes 1572872 | tf_op jit(solution)/shard_map/ppermute | solution.py:429
  272.7 1.8 collective-permute-start.14
  274.5 4.3 %collective-permute-start.15 = (bf16[4,128,256]{2,1,0:T(8,128)(2,1)S(1)}, bf16[4,128,256]{2,1,0:T(8,128)(2,1)S(1)}, u32[]{:S(2)}, u32[]{:S(2)}) collective-permute-start(bf16[4,128,256]{2,1,0:T(8,128)(2,1)S(1)} %collective-permute-done.10.refs_12_), channel_id=1, source_target_pairs={{0,16},{16,0},{32,48},{48,32},{64,80},{80,64},{96,112},{112,96},{1... | collective-permute-start | bytes 786440 | tf_op jit(solution)/shard_map/ppermute | solution.py:429
  278.8 1.1 collective-permute-done.15.refs_17_
  280.0 3.4 %copy-done.6 = bf16[16384,256]{1,0:T(8,128)(2,1)S(1)} copy-done((bf16[16384,256]{1,0:T(8,128)(2,1)S(1)}, bf16[16384,256]{1,0:T(8,128)(2,1)}, u32[]{:S(2)}) %copy-start.6) | copy-done | bytes 8388632
  283.4 1.0 copy-done.20
  284.4 19.8 %lab_step.1 = bf16[128,16,256]{2,1,0:T(8,128)(2,1)S(1)} custom-call(s32[1]{0:T(128)} %bitcast.row_ref, s32[8,128]{1,0:T(8,128)S(1)} %bitcast.45, bf16[2,64,16,128]{3,2,1,0:T(8,128)(2,1)S(1)} %copy-done.14, bf16[2,64,16,128]{3,2,1,0:T(8,128)(2,1)S(1)} %copy-done.16, bf16[2,64,16,128]{3,2,1,0:T(8,128)(2,1)S(1)} %copy-done.18, ...), custom_call_target="tpu_custom_call" | custom-call | tf_op jit(solution)/shard_map/lab_step/pallas_call | solution.py:516
  304.2 18.1 %all_to_all.83 = bf16[8,256,256]{2,1,0:T(8,128)(2,1)S(1)} all-to-all(bf16[8,256,256]{2,1,0:T(8,128)(2,1)S(1)} %bitcast.33), channel_id=1, replica_groups=mesh['rows'=8,'cols'=16] {'rows'}, dimensions={0} | all-to-all | bytes 2097152 | tf_op jit(solution)/shard_map/all_to_all | solution.py:535
  322.3 1.7 convert_add_fusion
  (84 shorter events, 13.1 us)
Async XLA Ops:
  7.2 60.2 %copy-start = (bf16[256,256]{1,0:T(8,128)(2,1)S(1)}, bf16[256,256]{1,0:T(8,128)(2,1)}, u32[]{:S(2)}) copy-start(bf16[256,256]{1,0:T(8,128)(2,1)} %param.17) | copy-start | bytes 393220
  7.2 25.3 %copy-start.30 = (s32[1,64]{1,0:T(1,128)S(1)}, s32[1,64]{1,0:T(1,128)}, u32[]{:S(2)}) copy-start(s32[1,64]{1,0:T(1,128)} %lab_ref.1) | copy-start | bytes 772
  7.2 25.3 %copy-start.29 = (s32[1,64]{1,0:T(1,128)S(1)}, s32[1,64]{1,0:T(1,128)}, u32[]{:S(2)}) copy-start(s32[1,64]{1,0:T(1,128)} %patient_ref.1) | copy-start | bytes 772
  7.2 74.6 %all-gather.3.cloned.1.call-start = ((), (), s32[]{:S(2)}) async-start(), calls=%async_computation.10 | async-start | bytes 9437184 | tf_op jit(solution)/shard_map/all_gather | solution.py:389
  32.5 1.6 copy-start.9
  34.1 1.6 copy-start.10
  35.7 31.1 %copy-start.12 = (bf16[1024,256]{1,0:T(8,128)(2,1)S(1)}, bf16[1024,256]{1,0:T(8,128)(2,1)}, u32[]{:S(2)}) copy-start(bf16[1024,256]{1,0:T(8,128)(2,1)} %param.10) | copy-start | bytes 1572868
  46.5 1.3 copy-start.7
  47.9 0.8 copy-start.13
  48.7 0.8 copy-start.31
  49.5 0.8 copy-start.32
  50.3 0.8 copy-start.33
  51.1 0.8 copy-start.34
  51.9 0.8 copy-start.35
  52.7 0.8 copy-start.36
  53.5 0.8 copy-start.37
  81.8 3.4 %copy-start.5 = (bf16[16384,256]{1,0:T(8,128)(2,1)S(1)}, bf16[16384,256]{1,0:T(8,128)(2,1)}, u32[]{:S(2)}) copy-start(bf16[16384,256]{1,0:T(8,128)(2,1)} %all-gather.3.cloned.1.call-done) | copy-start | bytes 25165828
  85.2 1.6 copy-start.8
  93.9 2.1 copy-start.1
  96.0 1.0 copy-start.11
  97.0 29.5 %all-to-all-start.1 = ((f32[16,64,256]{2,1,0:T(8,128)}), f32[16,64,256]{2,1,0:T(8,128)S(1)}, u32[]{:S(2)}, u32[]{:S(2)}) async-start(f32[16,64,256]{2,1,0:T(8,128)} %bitcast.43), calls=%async_computation.1 | async-start | bytes 2097152 | tf_op jit(solution)/shard_map/all_to_all | solution.py:447
  109.6 2.2 collective-permute-start
  109.7 13.4 %collective-permute-start.1 = (bf16[2,64,16,128]{3,2,1,0:T(8,128)(2,1)}, bf16[2,64,16,128]{3,2,1,0:T(8,128)(2,1)S(1)}, u32[]{:S(2)}, u32[]{:S(2)}) collective-permute-start(bf16[2,64,16,128]{3,2,1,0:T(8,128)(2,1)} %copy-done.36), channel_id=1, source_target_pairs={{0,32},{16,48},{32,0},{48,16},{64,96},{80,112},{96,64},{112,80},{1... | collective-permute-start | bytes 1572872 | tf_op jit(solution)/shard_map/ppermute | solution.py:429
  111.8 0.8 copy-start.15
  123.0 0.8 copy-start.17
  126.4 0.8 copy-start.23
  127.3 0.8 copy-start.24
  128.4 0.8 copy-start.21
  129.2 0.7 copy-start.25
  129.9 12.9 %all-to-all-start.2 = ((bf16[16,64,256]{2,1,0:T(8,128)(2,1)}), bf16[16,64,256]{2,1,0:T(8,128)(2,1)S(1)}, u32[]{:S(2)}, u32[]{:S(2)}) async-start(bf16[16,64,256]{2,1,0:T(8,128)(2,1)} %copy-done.21), calls=%async_computation.2 | async-start | bytes 1048576 | tf_op jit(solution)/shard_map/all_to_all | solution.py:452
  134.0 21.8 %collective-permute-start.2 = (bf16[2,64,16,128]{3,2,1,0:T(8,128)(2,1)}, bf16[2,64,16,128]{3,2,1,0:T(8,128)(2,1)S(1)}, u32[]{:S(2)}, u32[]{:S(2)}) collective-permute-start(bf16[2,64,16,128]{3,2,1,0:T(8,128)(2,1)} %copy-done.35), channel_id=1, source_target_pairs={{0,48},{16,32},{32,16},{48,0},{64,112},{80,96},{96,80},{112,64},{1... | collective-permute-start | bytes 1572872 | tf_op jit(solution)/shard_map/ppermute | solution.py:429
  135.5 24.8 %collective-permute-start.3 = (bf16[2,64,16,128]{3,2,1,0:T(8,128)(2,1)}, bf16[2,64,16,128]{3,2,1,0:T(8,128)(2,1)}, u32[]{:S(2)}, u32[]{:S(2)}) collective-permute-start(bf16[2,64,16,128]{3,2,1,0:T(8,128)(2,1)} %copy-done.34), channel_id=1, source_target_pairs={{0,64},{16,80},{32,96},{48,112},{64,0},{80,16},{96,32},{112,48},{1... | collective-permute-start | bytes 1572872 | tf_op jit(solution)/shard_map/ppermute | solution.py:429
  142.9 2.2 copy-start.2
  149.5 16.5 %all-to-all-start.3 = ((bf16[16,64,256]{2,1,0:T(8,128)(2,1)}), bf16[16,64,256]{2,1,0:T(8,128)(2,1)S(1)}, u32[]{:S(2)}, u32[]{:S(2)}) async-start(bf16[16,64,256]{2,1,0:T(8,128)(2,1)} %bitcast.11), calls=%async_computation.3 | async-start | bytes 1048576 | tf_op jit(solution)/shard_map/all_to_all | solution.py:447
  155.8 32.5 %copy-start.19 = (bf16[2,64,16,128]{3,2,1,0:T(8,128)(2,1)}, bf16[2,64,16,128]{3,2,1,0:T(8,128)(2,1)S(1)}, u32[]{:S(2)}) copy-start(bf16[2,64,16,128]{3,2,1,0:T(8,128)(2,1)S(1)} %collective-permute-done.2.refs_3_) | copy-start | bytes 1572868
  166.1 1.0 copy-start.26
  167.5 0.8 copy-start.22
  168.3 0.7 copy-start.27
  169.0 12.8 %all-to-all-start.4 = ((bf16[16,64,256]{2,1,0:T(8,128)(2,1)}), bf16[16,64,256]{2,1,0:T(8,128)(2,1)S(1)}, u32[]{:S(2)}, u32[]{:S(2)}) async-start(bf16[16,64,256]{2,1,0:T(8,128)(2,1)} %copy-done.22), calls=%async_computation.4 | async-start | bytes 1048576 | tf_op jit(solution)/shard_map/all_to_all | solution.py:452
  172.6 21.1 %collective-permute-start.4 = (bf16[2,64,16,128]{3,2,1,0:T(8,128)(2,1)}, bf16[2,64,16,128]{3,2,1,0:T(8,128)(2,1)}, u32[]{:S(2)}, u32[]{:S(2)}) collective-permute-start(bf16[2,64,16,128]{3,2,1,0:T(8,128)(2,1)} %copy-done.33), channel_id=1, source_target_pairs={{0,80},{16,64},{32,112},{48,96},{64,16},{80,0},{96,48},{112,32},{1... | collective-permute-start | bytes 1572872 | tf_op jit(solution)/shard_map/ppermute | solution.py:429
  175.3 25.0 %collective-permute-start.5 = (bf16[2,64,16,128]{3,2,1,0:T(8,128)(2,1)}, bf16[2,64,16,128]{3,2,1,0:T(8,128)(2,1)}, u32[]{:S(2)}, u32[]{:S(2)}) collective-permute-start(bf16[2,64,16,128]{3,2,1,0:T(8,128)(2,1)} %copy-done.32), channel_id=1, source_target_pairs={{0,96},{16,112},{32,64},{48,80},{64,32},{80,48},{96,0},{112,16},{1... | collective-permute-start | bytes 1572872 | tf_op jit(solution)/shard_map/ppermute | solution.py:429
  181.8 2.2 copy-start.3
  188.3 14.3 %all-to-all-start.5 = ((bf16[16,64,256]{2,1,0:T(8,128)(2,1)}), bf16[16,64,256]{2,1,0:T(8,128)(2,1)S(1)}, u32[]{:S(2)}, u32[]{:S(2)}) async-start(bf16[16,64,256]{2,1,0:T(8,128)(2,1)} %bitcast.13), calls=%async_computation.5 | async-start | bytes 1048576 | tf_op jit(solution)/shard_map/all_to_all | solution.py:447
  202.7 1.0 copy-start.28
  204.7 13.5 %all-to-all-start.6 = ((bf16[16,64,256]{2,1,0:T(8,128)(2,1)}), bf16[16,64,256]{2,1,0:T(8,128)(2,1)S(1)}, u32[]{:S(2)}, u32[]{:S(2)}) async-start(bf16[16,64,256]{2,1,0:T(8,128)(2,1)} %get-tuple-element.99), calls=%async_computation.6 | async-start | bytes 1048576 | tf_op jit(solution)/shard_map/all_to_all | solution.py:452
  209.0 21.1 %collective-permute-start.6 = (bf16[2,64,16,128]{3,2,1,0:T(8,128)(2,1)}, bf16[2,64,16,128]{3,2,1,0:T(8,128)(2,1)}, u32[]{:S(2)}, u32[]{:S(2)}) collective-permute-start(bf16[2,64,16,128]{3,2,1,0:T(8,128)(2,1)} %copy-done.31), channel_id=1, source_target_pairs={{0,112},{16,96},{32,80},{48,64},{64,48},{80,32},{96,16},{112,0},{1... | collective-permute-start | bytes 1572872 | tf_op jit(solution)/shard_map/ppermute | solution.py:429
  218.2 2.2 copy-start.4
  224.7 55.3 %copy-start.14 = (bf16[2,64,16,128]{3,2,1,0:T(8,128)(2,1)S(1)}, bf16[2,64,16,128]{3,2,1,0:T(8,128)(2,1)}, u32[]{:S(2)}) copy-start(bf16[2,64,16,128]{3,2,1,0:T(8,128)(2,1)} %copy-done.13) | copy-start | bytes 1572868
  224.7 55.3 %copy-start.16 = (bf16[2,64,16,128]{3,2,1,0:T(8,128)(2,1)S(1)}, bf16[2,64,16,128]{3,2,1,0:T(8,128)(2,1)}, u32[]{:S(2)}) copy-start(bf16[2,64,16,128]{3,2,1,0:T(8,128)(2,1)} %copy-done.15) | copy-start | bytes 1572868
  224.7 55.3 %copy-start.18 = (bf16[2,64,16,128]{3,2,1,0:T(8,128)(2,1)S(1)}, bf16[2,64,16,128]{3,2,1,0:T(8,128)(2,1)}, u32[]{:S(2)}) copy-start(bf16[2,64,16,128]{3,2,1,0:T(8,128)(2,1)} %copy-done.17) | copy-start | bytes 1572868
  224.7 14.6 %all-to-all-start.7 = ((bf16[16,64,256]{2,1,0:T(8,128)(2,1)}), bf16[16,64,256]{2,1,0:T(8,128)(2,1)S(1)}, u32[]{:S(2)}, u32[]{:S(2)}) async-start(bf16[16,64,256]{2,1,0:T(8,128)(2,1)} %bitcast.15), calls=%async_computation.7 | async-start | bytes 1048576 | tf_op jit(solution)/shard_map/all_to_all | solution.py:447
  252.2 10.2 %collective-permute-start.8 = (bf16[8,128,256]{2,1,0:T(8,128)(2,1)S(1)}, bf16[8,128,256]{2,1,0:T(8,128)(2,1)S(1)}, u32[]{:S(2)}, u32[]{:S(2)}) collective-permute-start(bf16[8,128,256]{2,1,0:T(8,128)(2,1)S(1)} %bitcast.34), channel_id=1, source_target_pairs={{0,96},{16,112},{32,64},{48,80},{64,32},{80,48},{96,0},{112,16},{1... | collective-permute-start | bytes 1572872 | tf_op jit(solution)/shard_map/ppermute | solution.py:429
  252.3 12.6 %collective-permute-start.7 = (bf16[8,128,256]{2,1,0:T(8,128)(2,1)S(1)}, bf16[8,128,256]{2,1,0:T(8,128)(2,1)S(1)}, u32[]{:S(2)}, u32[]{:S(2)}) collective-permute-start(bf16[8,128,256]{2,1,0:T(8,128)(2,1)S(1)} %bitcast.35), channel_id=1, source_target_pairs={{0,32},{16,48},{32,0},{48,16},{64,96},{80,112},{96,64},{112,80},{1... | collective-permute-start | bytes 1572872 | tf_op jit(solution)/shard_map/ppermute | solution.py:429
  256.0 22.8 %collective-permute-start.11 = (bf16[8,128,256]{2,1,0:T(8,128)(2,1)S(1)}, bf16[8,128,256]{2,1,0:T(8,128)(2,1)S(1)}, u32[]{:S(2)}, u32[]{:S(2)}) collective-permute-start(bf16[8,128,256]{2,1,0:T(8,128)(2,1)S(1)} %bitcast.36), channel_id=1, source_target_pairs={{0,16},{16,0},{32,48},{48,32},{64,80},{80,64},{96,112},{112,96},{1... | collective-permute-start | bytes 1572872 | tf_op jit(solution)/shard_map/ppermute | solution.py:429
  262.4 10.3 %collective-permute-start.9 = (bf16[4,128,256]{2,1,0:T(8,128)(2,1)S(1)}, bf16[4,128,256]{2,1,0:T(8,128)(2,1)S(1)}, u32[]{:S(2)}, u32[]{:S(2)}) collective-permute-start(bf16[4,128,256]{2,1,0:T(8,128)(2,1)S(1)} %slice.8), channel_id=1, source_target_pairs={{0,32},{16,48},{32,0},{48,16},{64,96},{80,112},{96,64},{112,80},{1... | collective-permute-start | bytes 786440 | tf_op jit(solution)/shard_map/ppermute | solution.py:429
  264.9 9.6 %collective-permute-start.10 = (bf16[4,128,256]{2,1,0:T(8,128)(2,1)S(1)}, bf16[4,128,256]{2,1,0:T(8,128)(2,1)S(1)}, u32[]{:S(2)}, u32[]{:S(2)}) collective-permute-start(bf16[4,128,256]{2,1,0:T(8,128)(2,1)S(1)} %slice.9), channel_id=1, source_target_pairs={{0,96},{16,112},{32,64},{48,80},{64,32},{80,48},{96,0},{112,16},{1... | collective-permute-start | bytes 786440 | tf_op jit(solution)/shard_map/ppermute | solution.py:429
  266.8 12.0 %collective-permute-start.13 = (bf16[8,128,256]{2,1,0:T(8,128)(2,1)S(1)}, bf16[8,128,256]{2,1,0:T(8,128)(2,1)S(1)}, u32[]{:S(2)}, u32[]{:S(2)}) collective-permute-start(bf16[8,128,256]{2,1,0:T(8,128)(2,1)S(1)} %collective-permute-done.8.refs_10_), channel_id=1, source_target_pairs={{0,16},{16,0},{32,48},{48,32},{64,80},{80,64},{96,112},{112,96},{1... | collective-permute-start | bytes 1572872 | tf_op jit(solution)/shard_map/ppermute | solution.py:429
  272.7 7.3 %collective-permute-start.12 = (bf16[8,128,256]{2,1,0:T(8,128)(2,1)S(1)}, bf16[8,128,256]{2,1,0:T(8,128)(2,1)S(1)}, u32[]{:S(2)}, u32[]{:S(2)}) collective-permute-start(bf16[8,128,256]{2,1,0:T(8,128)(2,1)S(1)} %collective-permute-done.7.refs_9_), channel_id=1, source_target_pairs={{0,16},{16,0},{32,48},{48,32},{64,80},{80,64},{96,112},{112,96},{1... | collective-permute-start | bytes 1572872 | tf_op jit(solution)/shard_map/ppermute | solution.py:429
  272.7 6.2 %collective-permute-start.14 = (bf16[4,128,256]{2,1,0:T(8,128)(2,1)S(1)}, bf16[4,128,256]{2,1,0:T(8,128)(2,1)S(1)}, u32[]{:S(2)}, u32[]{:S(2)}) collective-permute-start(bf16[4,128,256]{2,1,0:T(8,128)(2,1)S(1)} %collective-permute-done.9.refs_11_), channel_id=1, source_target_pairs={{0,16},{16,0},{32,48},{48,32},{64,80},{80,64},{96,112},{112,96},{1... | collective-permute-start | bytes 786440 | tf_op jit(solution)/shard_map/ppermute | solution.py:429
  274.5 5.5 %collective-permute-start.15 = (bf16[4,128,256]{2,1,0:T(8,128)(2,1)S(1)}, bf16[4,128,256]{2,1,0:T(8,128)(2,1)S(1)}, u32[]{:S(2)}, u32[]{:S(2)}) collective-permute-start(bf16[4,128,256]{2,1,0:T(8,128)(2,1)S(1)} %collective-permute-done.10.refs_12_), channel_id=1, source_target_pairs={{0,16},{16,0},{32,48},{48,32},{64,80},{80,64},{96,112},{112,96},{1... | collective-permute-start | bytes 786440 | tf_op jit(solution)/shard_map/ppermute | solution.py:429
  280.0 3.4 %copy-start.6 = (bf16[16384,256]{1,0:T(8,128)(2,1)S(1)}, bf16[16384,256]{1,0:T(8,128)(2,1)}, u32[]{:S(2)}) copy-start(bf16[16384,256]{1,0:T(8,128)(2,1)} %all-gather.3.cloned.1.call-done) | copy-start | bytes 25165828
  283.4 1.0 copy-start.20
  304.2 18.1 %copy-start.38 = (bf16[16,128,256]{2,1,0:T(8,128)(2,1)S(1)}, bf16[16,128,256]{2,1,0:T(8,128)(2,1)}, u32[]{:S(2)}) copy-start(bf16[16,128,256]{2,1,0:T(8,128)(2,1)} %all_to_all.81) | copy-start | bytes 3145732
Sparse Core Ops, SparseCore 0:
  31.9 49.7 all-gather.2

commit v2 on v1

v2 whole, which is shorter than its diff:
```python
import functools

import jax
import jax.numpy as jnp
from jax import lax
from jax.experimental import pallas as pl
from jax.experimental.pallas import tpu as pltpu
from jax.sharding import PartitionSpec as P

ITERS = 3
ridge_term = 1.0
highest = lax.Precision.HIGHEST
bf16 = jnp.bfloat16
f32 = jnp.float32
MIB = 1 << 20
BIG = 56

VMEM = pl.BlockSpec(memory_space=pltpu.VMEM)
SMEM = pl.BlockSpec(memory_space=pltpu.SMEM)
ANY = pl.BlockSpec(memory_space=pl.ANY)

GROUP = 8
SIDE = 4
PASS_TYPES = (f32, bf16)


def dot_nt(a, b):
    return lax.dot_general(a, b, (((1,), (1,)), ((), ())), preferred_element_type=f32)


def dot_nn(a, b):
    return lax.dot_general(a, b, (((1,), (0,)), ((), ())), preferred_element_type=f32)


def prep_kernel(
    tiles, slots, row_ref, patient_ref, lab_ref, count_ref, x_ref, w_ref, meta_ref, work_ref, xs_ref, ws_ref, *rest
):
    same, other, tmp, order, fill = rest[:-4], rest[-4], rest[-3], rest[-2], rest[-1]
    n = 2 * len(same)
    share = x_ref.shape[2] // n
    live = count_ref[0, 0]
    row = row_ref[0]

    def clear(i, carry):
        meta_ref[0, i] = 0
        return carry

    lax.fori_loop(0, meta_ref.shape[1], clear, 0)
    for p in range(tiles + 2):
        fill[p] = 0

    def key_of(s):
        return jnp.where(s < live, patient_ref[0, s], tiles)

    def count(s, carry):
        key = key_of(s)
        fill[key + 1] = fill[key + 1] + 1
        return carry

    lax.fori_loop(0, slots, count, 0)
    for p in range(tiles + 1):
        fill[p + 1] = fill[p + 1] + fill[p]
        meta_ref[0, slots + p] = fill[p]

    def place(s, carry):
        key = key_of(s)
        at = fill[key]
        fill[key] = at + 1
        order[at] = s
        meta_ref[0, at] = lab_ref[0, s]
        return carry

    lax.fori_loop(0, slots, place, 0)

    def no_work(i, carry):
        for f in range(4):
            work_ref[f, i] = 0
        return carry

    lax.fori_loop(0, work_ref.shape[1], no_work, 0)
    chunks = jnp.int32(0)
    for p in range(tiles):
        lo, hi = meta_ref[0, slots + p], meta_ref[0, slots + p + 1]

        def add(i, carry, p=p, lo=lo, hi=hi, chunks=chunks):
            work_ref[0, chunks + i] = p
            work_ref[1, chunks + i] = lo + i * GROUP
            work_ref[2, chunks + i] = hi
            return carry

        count_p = (hi - lo + GROUP - 1) // GROUP
        lax.fori_loop(0, count_p, add, 0)
        chunks = chunks + count_p

    def pad(i, carry):
        work_ref[2, i] = live
        work_ref[1, i] = live
        return carry

    blocks = (chunks + SIDE - 1) // SIDE
    lax.fori_loop(chunks, blocks * SIDE, pad, 0)
    work_ref[3, 0] = blocks

    size = x_ref.shape[1]
    eye = (
        lax.broadcasted_iota(jnp.int32, (size, size), 0)
        == lax.broadcasted_iota(jnp.int32, (size, size), 1)
    ).astype(f32).astype(bf16)

    def turn(i, carry):
        for u in range(2):
            s = i * 2 + u
            src = order[s]
            vals, wts = x_ref[src], w_ref[src]
            xs_ref[s] = vals
            ws_ref[s] = wts
            tmp[u, 0] = dot_nt(eye, vals).astype(bf16)
            tmp[u, 1] = dot_nt(eye, wts).astype(bf16)
        for u in range(2):
            s = i * 2 + u
            for k in range(n):
                at = pl.multiple_of((row ^ k) * share, share)
                to = same[k // 2] if k % 2 == 0 else other.at[k // 2]
                to[0, s] = tmp[u, 0, pl.ds(at, share), :]
                to[1, s] = tmp[u, 1, pl.ds(at, share), :]
        return carry

    lax.fori_loop(0, slots // 2, turn, 0)


def patient_sums(with_values, work_ref, x_ref, w_ref, v_ref, y_ref, out_ref, acc, arrive):
    acc[...] = jnp.zeros_like(acc)

    def chunk(c):
        tile, first, end = [work_ref[f, c] for f in range(3)]
        at = [jnp.maximum(jnp.minimum(first + j, end - 1), 0) for j in range(GROUP)]
        labs = jnp.concatenate([v_ref[a] for a in at], axis=0)
        wts = jnp.concatenate(
            [w_ref[a].astype(f32) * (first + j < end).astype(f32) for j, a in enumerate(at)], axis=1
        )
        scores = dot_nt(y_ref[tile], labs)
        if with_values:
            vals = jnp.concatenate([x_ref[a].astype(f32) for a in at], axis=1)
            kern = wts * (vals - scores)
        else:
            kern = wts * scores
        return tile, dot_nn(kern.astype(bf16), labs)

    def block(b, there):
        there = arrive(there, work_ref[2, b * SIDE + SIDE - 1])
        found = [chunk(b * SIDE + j) for j in range(SIDE)]
        for tile, terms in found:
            acc[tile] += terms
        return there

    lax.fori_loop(0, work_ref[3, 0], block, jnp.int32(1))
    out_ref[...] = acc[...].astype(out_ref.dtype)


def first_pass_kernel(slots, meta_ref, work_ref, *refs):
    xs_any, ws_any, lab_any, y_ref, out_ref, kept_any = refs[:6]
    v_ref, w_ref, acc, v_sem, w_sem, x_ref, x_sem, kept_sem = refs[6:]
    live = meta_ref[0, slots + y_ref.shape[0]]
    batches = (live + GROUP - 1) // GROUP

    def at(c):
        return pl.ds(c * GROUP, GROUP)

    def keep(c):
        return pltpu.make_async_copy(v_ref.at[at(c)], kept_any.at[at(c)], kept_sem.at[c])

    def rest(c, waited):
        copies = [
            pltpu.make_async_copy(ws_any.at[at(c)], w_ref.at[at(c)], w_sem.at[c]),
            pltpu.make_async_copy(xs_any.at[at(c)], x_ref.at[at(c)], x_sem.at[c]),
        ]
        if waited:
            copies.append(
                pltpu.make_async_copy(lab_any.at[pl.ds(0, GROUP)], v_ref.at[at(c)], v_sem.at[c])
            )
        return copies

    def start(c, carry):
        for j in range(GROUP):
            s = c * GROUP + j
            pltpu.make_async_copy(lab_any.at[meta_ref[0, s]], v_ref.at[s], v_sem.at[c]).start()
        for copy in rest(c, False):
            copy.start()
        return carry

    lax.fori_loop(0, batches, start, 0)

    def wait(c, carry):
        for copy in rest(c, True):
            copy.wait()
        keep(c).start()
        return carry

    wait(0, 0)

    def arrive(there, hi):
        until = jnp.maximum((hi + GROUP - 1) // GROUP, there)
        lax.fori_loop(there, until, wait, 0)
        return until

    patient_sums(True, work_ref, x_ref, w_ref, v_ref, y_ref, out_ref, acc, arrive)

    def end(c, carry):
        keep(c).wait()
        return carry

    lax.fori_loop(0, batches, end, 0)


def pass_kernel(work_ref, w_ref, v_ref, y_ref, out_ref, acc):
    patient_sums(
        False, work_ref, None, w_ref, v_ref, y_ref, out_ref, acc, lambda there, hi: there
    )


def spread(probe_ref, rows):
    for k in range(probe_ref.shape[0]):
        probe_ref[k] = rows


def first_kernel(recv_ref, start_ref, side_ref, gram_ref, state_ref, probe_ref):
    residual = jnp.sum(recv_ref[...].astype(f32), axis=0) + side_ref[...]
    state_ref[0] = start_ref[...].astype(f32)
    state_ref[1] = residual
    state_ref[2] = residual
    state_ref[3] = (
        jnp.dot(residual, gram_ref[...], precision=highest, preferred_element_type=f32)
        + ridge_term * residual
    )
    spread(probe_ref, residual.astype(bf16))


def step_kernel(turn_ref, recv_ref, state_in, gram_ref, state_ref, probe_ref):
    residual = state_in[1]
    direction = state_in[2]
    applied = jnp.sum(recv_ref[...].astype(f32), axis=0) + state_in[3]
    norm_now = jnp.sum(residual * residual, axis=1, keepdims=True)
    step_size = norm_now / jnp.sum(direction * applied, axis=1, keepdims=True)
    solution_now = state_in[0] + step_size * direction
    state_ref[0] = solution_now
    last = turn_ref[0] == ITERS - 1

    @pl.when(last)
    def _():
        spread(probe_ref, solution_now.astype(bf16))

    @pl.when(jnp.logical_not(last))
    def _():
        residual_next = residual - step_size * applied
        norm_next = jnp.sum(residual_next * residual_next, axis=1, keepdims=True)
        direction_next = residual_next + norm_next / norm_now * direction
        state_ref[1] = residual_next
        state_ref[2] = direction_next
        state_ref[3] = (
            jnp.dot(
                direction_next, gram_ref[...], precision=highest, preferred_element_type=f32
            )
            + ridge_term * direction_next
        )
        spread(probe_ref, direction_next.astype(bf16))


def lab_kernel(slots, n, row_ref, meta_ref, *refs):
    pieces, refs = refs[: n // 2], refs[n // 2 :]
    f_own, f_two, f_six, f_top, f_low, g_own, g_two, g_six, g_top, g_low = refs[:10]
    lab_any, out_ref, xw, f_ref, v_ref, acc, probe, curv, p_sem, f_sem, v_sem = refs[10:]
    tiles = f_ref.shape[0] // n
    half = tiles // 2
    share = v_ref.shape[1]
    size = f_ref.shape[1]
    row = row_ref[0]
    v_copy = pltpu.make_async_copy(lab_any.at[:, row], v_ref, v_sem)
    v_copy.start()
    factors = {0: [f_own], 1: [g_own], 2: [f_two], 3: [g_two], 6: [f_six], 7: [g_six]}
    factors |= {4: [f_top, f_low], 5: [g_top, g_low]}
    for k in range(n):
        pltpu.make_async_copy(pieces[k // 2].at[k % 2], xw.at[k], p_sem.at[k]).start()
        for h, ref in enumerate(factors[k]):
            to = pl.ds((row ^ k) * tiles + h * half, ref.shape[0])
            pltpu.make_async_copy(ref, f_ref.at[to], f_sem.at[k]).start()
    acc[...] = jnp.zeros_like(acc)
    curv[...] = jnp.zeros_like(curv)
    v_copy.wait()

    span = GROUP * share
    row_slot = lax.broadcasted_iota(jnp.int32, (span, size), 0) // share

    def sweep(terms_of, total, arrive):
        def of_source(k, carry):
            source = row ^ k
            arrive(k, source)
            lo = [meta_ref[source, slots + p] for p in range(tiles)]
            hi = [meta_ref[source, slots + p + 1] for p in range(tiles)]

            def block(i, carry):
                found = []
                for p in range(tiles):
                    first = lo[p] + i * GROUP
                    base = jnp.minimum(first, slots - GROUP)
                    labs = [meta_ref[source, base + j] for j in range(GROUP)]
                    inside = (row_slot >= first - base) & (row_slot < hi[p] - base)
                    wts = xw[k, 1, pl.ds(base, GROUP)].reshape(span, size).astype(f32)
                    wts = jnp.where(inside, wts, 0.0)
                    found.append((labs, terms_of(k, base, labs, wts, f_ref[source * tiles + p])))
                for labs, terms in found:
                    for j, t in enumerate(labs):
                        total[t] += terms[j * share : (j + 1) * share]
                return carry

            most = functools.reduce(jnp.maximum, [b - a for a, b in zip(lo, hi)])
            return lax.fori_loop(0, (most + GROUP - 1) // GROUP, block, carry)

        lax.fori_loop(0, n, of_source, 0)

    def residual_terms(k, base, labs, wts, patients):
        rows = jnp.concatenate([v_ref[t] for t in labs], axis=0)
        vals = xw[k, 0, pl.ds(base, GROUP)].reshape(span, size).astype(f32)
        return dot_nn((wts * (vals - dot_nt(rows, patients))).astype(bf16), patients)

    def arrive(k, source):
        pltpu.make_async_copy(xw.at[0], xw.at[k], p_sem.at[k]).wait()
        at = pl.ds(source * tiles, tiles)
        pltpu.make_async_copy(f_ref.at[pl.ds(0, tiles)], f_ref.at[at], f_sem.at[k]).wait()

    sweep(residual_terms, acc, arrive)

    block = 16

    def finish(i, carry):
        at = pl.ds(i * block, block)
        rest = acc[at] - ridge_term * v_ref[at].astype(f32)
        acc[at] = rest
        probe[at] = rest.astype(bf16)
        return carry

    lax.fori_loop(0, acc.shape[0] // block, finish, 0)

    def curvature_terms(k, base, labs, wts, patients):
        rows = jnp.concatenate([probe[t] for t in labs], axis=0)
        inner = dot_nt(rows, patients)
        return wts * inner * inner

    sweep(curvature_terms, curv, lambda k, source: None)

    def emit(i, carry):
        at = pl.ds(i * block, block)
        rest = acc[at]
        norm = jnp.sum(rest * rest, axis=-1, keepdims=True)
        total = jnp.sum(curv[at], axis=-1, keepdims=True) + ridge_term * norm
        out_ref[at] = (norm / total * rest).astype(out_ref.dtype)
        return carry

    lax.fori_loop(0, acc.shape[0] // block, emit, 0)


def shape_of(shape, dtype):
    return jax.ShapeDtypeStruct(shape, dtype)


def params(mib):
    return pltpu.CompilerParams(vmem_limit_bytes=mib * MIB)


def shards(
    lab_factors,
    patient_factors,
    values,
    weights,
    tile_patient,
    tile_lab,
    tile_count,
    ecg_embed,
    ecg_map,
):
    rows = lax.axis_size("rows")
    cols = lax.axis_size("cols")
    size = values.shape[2]
    slots = values.shape[1]
    rank = lab_factors.shape[1]
    owned_tiles = lab_factors.shape[0] // size
    col_tiles = owned_tiles * rows
    patient_rows = patient_factors.shape[0]
    tiles = patient_rows // size
    share_rows = patient_rows // cols
    lab_share = size // rows
    row = lax.axis_index("rows").astype(jnp.int32).reshape(1)
    x, w = values[0], weights[0]

    own_labs = lax.all_to_all(lab_factors, "cols", split_axis=0, concat_axis=0, tiled=True)
    labs = lax.all_gather(own_labs, "rows", axis=0, tiled=True)

    slot_shape = shape_of((slots, size, size), bf16)
    piece = (2, slots, lab_share, size)
    out_pieces = [shape_of(piece, bf16)] * (rows // 2) + [shape_of((rows // 2, *piece), bf16)]
    prep = pl.pallas_call(
        functools.partial(prep_kernel, tiles, slots),
        out_shape=[shape_of((1, 128), jnp.int32), shape_of((4, 128), jnp.int32)]
        + [slot_shape] * 2
        + out_pieces,
        in_specs=[SMEM] * 4 + [VMEM] * 2,
        out_specs=[SMEM] * 2 + [VMEM] * (2 + len(out_pieces)),
        scratch_shapes=[
            pltpu.VMEM((2, 2, size, size), bf16),
            pltpu.SMEM((slots,), jnp.int32),
            pltpu.SMEM((tiles + 2,), jnp.int32),
        ],
        compiler_params=params(BIG),
        name="prep",
    )(row, tile_patient, tile_lab, tile_count, x, w)
    (meta, work, xs, ws), same, other = prep[:4], prep[4:-1], prep[-1]

    def swap(array, k):
        return lax.ppermute(array, "rows", [(i, i ^ k) for i in range(rows)])

    other = swap(other, 1)
    pieces = [jnp.stack([same[h], other[h]]) for h in range(rows // 2)]
    meta_all = lax.all_gather(meta, "rows", axis=0, tiled=True)

    embed_map = ecg_map.astype(f32)
    gram = jnp.dot(embed_map.T, embed_map, precision=highest)
    share_at = lax.axis_index("cols") * share_rows
    start_share = lax.dynamic_slice_in_dim(patient_factors, share_at, share_rows).astype(f32)
    embed_share = lax.dynamic_slice_in_dim(ecg_embed, share_at, share_rows).astype(f32)
    side = (
        jnp.dot(
            embed_share - jnp.dot(start_share, embed_map.T, precision=highest),
            embed_map,
            precision=highest,
        )
        - ridge_term * start_share
    )

    labs, pieces, meta_all, side, gram, start_share = lax.optimization_barrier(
        (labs, pieces, meta_all, side, gram, start_share)
    )
    lab_tiles = labs.reshape(col_tiles, size, rank)

    pieces = [pieces[0]] + [swap(pieces[h], 2 * h) for h in range(1, rows // 2)]

    def exchange(partial):
        partial = partial.reshape(patient_rows, rank)
        recv = lax.all_to_all(partial, "cols", split_axis=0, concat_axis=0, tiled=True)
        return recv.reshape(cols, share_rows, rank)

    def to_all(probe):
        probe = probe.reshape(patient_rows, rank)
        probe = lax.all_to_all(probe, "cols", split_axis=0, concat_axis=0, tiled=True)
        return probe.reshape(tiles, size, rank)

    state_shape = shape_of((4, share_rows, rank), f32)
    probe_shape = shape_of((cols, share_rows, rank), bf16)
    batches = slots // GROUP
    partial, slot_labs = pl.pallas_call(
        functools.partial(first_pass_kernel, slots),
        out_shape=[
            shape_of((tiles, size, rank), PASS_TYPES[0]),
            shape_of((slots, size, rank), bf16),
        ],
        in_specs=[SMEM] * 2 + [ANY] * 3 + [VMEM],
        out_specs=[VMEM, ANY],
        scratch_shapes=[
            pltpu.VMEM((slots, size, rank), bf16),
            pltpu.VMEM((slots, size, size), bf16),
            pltpu.VMEM((tiles, size, rank), f32),
            pltpu.SemaphoreType.DMA((batches,)),
            pltpu.SemaphoreType.DMA((batches,)),
            pltpu.VMEM((slots, size, size), bf16),
            pltpu.SemaphoreType.DMA((batches,)),
            pltpu.SemaphoreType.DMA((batches,)),
        ],
        compiler_params=params(BIG),
        name="first_pass",
    )(meta, work, xs, ws, lab_tiles, patient_factors.reshape(tiles, size, rank))
    state, probe = pl.pallas_call(
        first_kernel,
        out_shape=[state_shape, probe_shape],
        in_specs=[VMEM] * 4,
        out_specs=[VMEM] * 2,
        compiler_params=params(8),
        name="first_step",
    )(exchange(partial), start_share, side, gram)

    def turn(iteration, carry):
        state, probe = carry
        partial = pl.pallas_call(
            pass_kernel,
            out_shape=shape_of((tiles, size, rank), PASS_TYPES[1]),
            in_specs=[SMEM] + [VMEM] * 3,
            out_specs=VMEM,
            scratch_shapes=[pltpu.VMEM((tiles, size, rank), f32)],
            compiler_params=params(16),
            name="patient_pass",
        )(work, ws, slot_labs, to_all(probe))
        state, probe = pl.pallas_call(
            step_kernel,
            out_shape=[state_shape, probe_shape],
            in_specs=[SMEM] + [VMEM] * 3,
            out_specs=[VMEM] * 2,
            compiler_params=params(8),
            name="step",
        )(iteration.reshape(1), exchange(partial), state, gram)
        return state, probe

    state, probe = lax.fori_loop(0, ITERS, turn, (state, probe))
    patient_out = state[0]

    f_own = to_all(probe)
    half = tiles // 2
    f_two, f_six = swap(f_own, 2), swap(f_own, 6)
    f_top, f_low = swap(f_six[:half], 2), swap(f_two[half:], 6)
    here = [f_own, f_two, f_six, f_top, f_low]
    factors = here + [swap(part, 1) for part in here]
    delta = pl.pallas_call(
        functools.partial(lab_kernel, slots, rows),
        out_shape=shape_of((col_tiles, lab_share, rank), bf16),
        in_specs=[SMEM] * 2 + [ANY] * (len(pieces) + len(factors) + 1),
        out_specs=VMEM,
        scratch_shapes=[
            pltpu.VMEM((rows, 2, slots, lab_share, size), bf16),
            pltpu.VMEM((rows * tiles, size, rank), bf16),
            pltpu.VMEM((col_tiles, lab_share, rank), bf16),
            pltpu.VMEM((col_tiles, lab_share, rank), f32),
            pltpu.VMEM((col_tiles, lab_share, rank), bf16),
            pltpu.VMEM((col_tiles, lab_share, size), f32),
            pltpu.SemaphoreType.DMA((rows,)),
            pltpu.SemaphoreType.DMA((rows,)),
            pltpu.SemaphoreType.DMA,
        ],
        compiler_params=params(BIG),
        name="lab_step",
    )(row, meta_all, *pieces, *factors, lab_tiles.reshape(col_tiles, rows, lab_share, rank))
    back = lax.all_to_all(
        delta.reshape(col_tiles * lab_share, rank), "rows", split_axis=0, concat_axis=0, tiled=True
    )
    back = back.reshape(rows, owned_tiles, lab_share, rank).transpose(1, 0, 2, 3)
    updated = own_labs.reshape(owned_tiles, rows, lab_share, rank).astype(f32) + back.astype(f32)
    return (patient_out, updated.reshape(1, owned_tiles * size, rank))


def solution(mesh):
    in_specs = (
        P(("rows", "cols"), None),
        P("rows", None),
        P("rows", "cols", None, None),
        P("rows", "cols", None, None),
        P("rows", "cols"),
        P("rows", "cols"),
        P("rows", "cols"),
        P("rows", None),
        P(),
    )
    out_specs = (P(("rows", "cols"), None), P("cols", "rows", None))
    return jax.shard_map(shards, mesh=mesh, in_specs=in_specs, out_specs=out_specs, check_vma=False)
```

time: 334 us -> 308 us (0.922)
  local copies, waits for them, and re-layouts: 38.2 us -> 4.44 us
  starting transfers between devices: 74 us -> 42.3 us
  blocking collectives: 67.2 us -> 88.8 us
  Pallas kernels: 53.6 us -> 63 us
  waiting for transfers between devices: 78.6 us -> 83.4 us
    all_to_all x1 -> x4, blocking collectives: 12.1 us -> 53.4 us  [to_all(): lax.all_to_all(probe, 'cols', split_axis=0, concat_axis=0, tiled=True)]
    unnamed x78 -> x32, local copies, waits for them, and re-layouts: 38.1 us -> 0.87 us
    all_to_all x4, waiting for transfers between devices: 20 us -> 41.2 us  [exchange(): lax.all_to_all(partial, 'cols', split_axis=0, concat_axis=0, tiled=True)]
    all_to_all x1 -> x0, blocking collectives: 18.1 us -> none  [shards(): lax.all_to_all(delta.reshape(col_tiles * lab_share, rank), 'rows', split_...]
    ppermute x16 -> x13, starting transfers between devices: 32.5 us -> 18.5 us  [swap(): return lax.ppermute(array, 'rows', [(i, i ^ k) for i in range(rows)])]
    ppermute x16 -> x13, waiting for transfers between devices: 27.1 us -> 16.8 us  [swap(): return lax.ppermute(array, 'rows', [(i, i ^ k) for i in range(rows)])]
    all_to_all x4, starting transfers between devices: 29.6 us -> 19.8 us  [exchange(): lax.all_to_all(partial, 'cols', split_axis=0, concat_axis=0, tiled=True)]
    all_to_all x3 -> x1, starting transfers between devices: 11.9 us -> 3.97 us  [shards(): lax.all_to_all(delta.reshape(col_tiles * lab_share, rank), 'rows', split_...]
  transfers between devices with their start and end apart: 24 -> 19, of which waited for: 14 -> 10; matrix products, arithmetic and copies ran while one was open for 1% -> 3% of each run, Pallas kernels for 7% -> 13%
where the time goes in v2:
time: 308 us; the launch traced here: 305 us
  blocking collectives  88.8 us (29%)
  waiting for transfers between devices  83.4 us (27%)
  Pallas kernels  63 us (20%)
  starting transfers between devices  42.3 us (14%)
  between operations  15 us (5%)
  other arithmetic  5.48 us (2%)
  local copies, waits for them, and re-layouts  4.44 us (1%)
    all_to_all x4, blocking collectives, to_all(): lax.all_to_all(probe, 'cols', split_axis=0, concat_axis=0, tiled=True)  53.4 us
    all_to_all x4, waiting for transfers between devices, exchange(): lax.all_to_all(partial, 'cols', split_axis=0, concat_axis=0, tiled=True)  41.2 us
    all_to_all x1, blocking collectives, shards(): lax.all_to_all(lab_factors, 'cols', split_axis=0, concat_axis=0, tiled=True)  24.4 us
    all_to_all x4, starting transfers between devices, exchange(): lax.all_to_all(partial, 'cols', split_axis=0, concat_axis=0, tiled=True)  19.8 us
    ppermute x13, starting transfers between devices, swap(): return lax.ppermute(array, 'rows', [(i, i ^ k) for i in range(rows)])  18.5 us
    pallas_call x1, Pallas kernels, shards(): pl.pallas_call(functools.partial(lab_kernel, slots, rows), out_shape=shap...  18.1 us
    pallas_call x3, Pallas kernels, turn(): pl.pallas_call(pass_kernel, out_shape=shape_of((tiles, size, rank), PASS_...  16.8 us
    ppermute x13, waiting for transfers between devices, swap(): return lax.ppermute(array, 'rows', [(i, i ^ k) for i in range(rows)])  16.8 us
  transfers between devices with their start and end apart: 19, of which 10 were waited for; matrix products, arithmetic and copies ran while one was open for 3% of the time, Pallas kernels for 13%

profile of v2, /device:TPU:1, one launch (start us, length us, event | category | flops | bytes accessed | tf_op | source)
XLA Modules:
  0.0 305.3 jit_solution(17684984239254995920)
XLA Ops:
  7.2 0.0 copy-start
  7.2 0.0 all-gather.3.cloned.1.call-start
  7.2 24.4 %all_to_all.60 = bf16[16,128,256]{2,1,0:T(8,128)(2,1)} all-to-all(bf16[16,128,256]{2,1,0:T(8,128)(2,1)} %bitcast.54), channel_id=1, replica_groups=mesh['rows'=8,'cols'=16] {'cols'}, dimensions={0} | all-to-all | bytes 2097152 | tf_op jit(solution)/shard_map/all_to_all | solution.py:394
  31.6 0.0 all-gather.3.cloned.1.call-update
  32.3 15.8 %prep.1 = (s32[1,128]{1,0:T(1,128)}, s32[4,128]{1,0:T(4,128)S(1)}, bf16[64,128,128]{2,1,0:T(8,128)(2,1)}, bf16[64,128,128]{2,1,0:T(8,128)(2,1)S(1)}, bf16[2,64,1...) custom-call(s32[1]{0:T(128)} %bitcast.3.row_ref, ...), custom_call_target="tpu_custom_call" | custom-call | tf_op jit(solution)/shard_map/prep/pallas_call | solution.py:400
  48.1 2.0 collective-permute-start
  50.1 11.0 %all-gather = s32[8,1,128]{2,1,0:T(1,128)} all-gather(s32[1,1,128]{2,1,0:T(1,128)} %bitcast.62), channel_id=1, replica_groups=mesh['rows'=8,'cols'=16] {'rows'}, dimensions={0}, use_global_device_ids=true | all-gather | bytes 4608 | tf_op jit(solution)/shard_map/all_gather | solution.py:422
  61.1 0.8 dynamic-slice_convert_fusion.start_ref
  61.9 0.9 convolution_subtract_fusion.1
  62.8 1.0 convolution_subtract_fusion.side_ref
  63.8 0.9 fusion.3.gram_ref
  64.8 2.0 fusion.2
  66.8 1.5 pad_maximum_fusion.2
  68.3 1.5 pad_maximum_fusion
  69.8 11.8 %all-gather.3.cloned.1.call-done = bf16[16384,256]{1,0:T(8,128)(2,1)} async-done(((bf16[2048,256]{1,0:T(8,128)(2,1)}), bf16[16384,256]{1,0:T(8,128)(2,1)}) %all-gather.3.cloned.1.call-update) | async-done | bytes 8388624 | tf_op jit(solution)/shard_map/all_gather | solution.py:395
  81.6 6.4 %first_pass.1 = (f32[8,128,256]{2,1,0:T(8,128)}, bf16[64,128,256]{2,1,0:T(8,128)(2,1)}) custom-call(s32[1,128]{1,0:T(1,128)} %get-tuple-element.144.meta_ref, s32[4,128]{1,0:T(4,128)S(1)} %get-tuple-element.240.work_ref, bf16[64,128,128]{2,1,0:T(8,128)(2,1)} %get-tuple-element.146.refs_0_, bf16[64,128,128]{2,1,0:T(8,128)(2,1)S(1)} %get-tuple-element.241.refs_1_, ...), custom_call_target="tpu_custom_call" | custom-call | tf_op jit(solution)/shard_map/first_pass/pallas_call | solution.py:458
  88.0 8.9 %all-to-all-start.3 = ((f32[16,64,256]{2,1,0:T(8,128)}), f32[16,64,256]{2,1,0:T(8,128)S(1)}, u32[]{:S(2)}, u32[]{:S(2)}) async-start(f32[16,64,256]{2,1,0:T(8,128)} %bitcast.55), calls=%async_computation.3 | async-start | bytes 2097152 | tf_op jit(solution)/shard_map/all_to_all | solution.py:447
  96.9 0.1 collective-permute-start.1
  97.0 0.1 collective-permute-start.2
  97.1 3.8 %collective-permute-start.3 = (bf16[2,2,64,16,128]{4,3,2,1,0:T(8,128)(2,1)}, bf16[2,2,64,16,128]{4,3,2,1,0:T(8,128)(2,1)}, u32[]{:S(2)}, u32[]{:S(2)}) collective-permute-start(bf16[2,2,64,16,128]{4,3,2,1,0:T(8,128)(2,1)} %get-tuple-element.166), channel_id=1, source_target_pairs={{0,96},{16,112},{32,64},{48,80},{64,32},{80,48},{96,0},{112,16},{1... | collective-permute-start | bytes 3145736 | tf_op jit(solution)/shard_map/ppermute | solution.py:418
  100.8 13.1 %all-to-all-done.3.recv_ref = f32[16,64,256]{2,1,0:T(8,128)S(1)} async-done(((f32[16,64,256]{2,1,0:T(8,128)}), f32[16,64,256]{2,1,0:T(8,128)S(1)}, u32[]{:S(2)}, u32[]{:S(2)}) %all-to-all-start.3) | async-done | bytes 1048608 | tf_op jit(solution)/shard_map/all_to_all | solution.py:447
  113.9 2.0 first_step.1
  115.9 100.8 %while.15 = (s32[]{:T(128)}, f32[4,64,256]{2,1,0:T(8,128)}, bf16[16,64,256]{2,1,0:T(8,128)(2,1)}, s32[4,128]{1,0:T(4,128)S(1)}, bf16[64,128,128]{2,1,0:T(8,128)(...) while((s32[]{:T(128)}, f32[4,64,256]{2,1,0:T(8,128)}, ...), condition=%wide.region_1.0_spmd, body=%wide.region_0.0_spmd.sunk | while | flops 2 | bytes 5243061 | solution.py:509
  115.9 15.5 %all_to_all.62 = bf16[16,64,256]{2,1,0:T(8,128)(2,1)S(1)} all-to-all(bf16[16,64,256]{2,1,0:T(8,128)(2,1)} %get-tuple-element.247), channel_id=1, replica_groups=mesh['rows'=8,'cols'=16] {'cols'}, dimensions={0} | all-to-all | bytes 1048576 | tf_op jit(solution)/shard_map/while/body/eval_jaxpr/all_to_all | solution.py:452
  131.4 5.6 %patient_pass.5 = bf16[8,128,256]{2,1,0:T(8,128)(2,1)} custom-call(s32[4,128]{1,0:T(4,128)S(1)} %get-tuple-element.256.work_ref, bf16[64,128,128]{2,1,0:T(8,128)(2,1)S(1)} %get-tuple-element.257.w_ref, bf16[64,128,256]{2,1,0:T(8,128)(2,1)} %get-tuple-element.258.v_ref, bf16[8,128,256]{2,1,0:T(8,128)(2,1)S(1)} %bitcast.40), custom_call_target="tpu_custom_call" | custom-call | tf_op jit(solution)/shard_map/while/body/eval_jaxpr/patient_pass/pallas_call | solution.py:490
  137.0 3.6 %all-to-all-start.1 = ((bf16[16,64,256]{2,1,0:T(8,128)(2,1)}), bf16[16,64,256]{2,1,0:T(8,128)(2,1)S(1)}, u32[]{:S(2)}, u32[]{:S(2)}) async-start(bf16[16,64,256]{2,1,0:T(8,128)(2,1)} %bitcast.39), calls=%async_computation.1 | async-start | bytes 1048576 | tf_op jit(solution)/shard_map/while/body/eval_jaxpr/all_to_all | solution.py:447
  140.6 10.3 %all-to-all-done.1.recv_ref = bf16[16,64,256]{2,1,0:T(8,128)(2,1)S(1)} async-done(((bf16[16,64,256]{2,1,0:T(8,128)(2,1)}), bf16[16,64,256]{2,1,0:T(8,128)(2,1)S(1)}, u32[]{:S(2)}, u32[]{:S(2)}) %all-to-all-start.1) | async-done | bytes 524320 | tf_op jit(solution)/shard_map/while/body/eval_jaxpr/all_to_all | solution.py:447
  150.9 1.4 step.5
  152.3 12.8 %all_to_all.62 = bf16[16,64,256]{2,1,0:T(8,128)(2,1)S(1)} all-to-all(bf16[16,64,256]{2,1,0:T(8,128)(2,1)} %get-tuple-element.247), channel_id=1, replica_groups=mesh['rows'=8,'cols'=16] {'cols'}, dimensions={0} | all-to-all | bytes 1048576 | tf_op jit(solution)/shard_map/while/body/eval_jaxpr/all_to_all | solution.py:452
  165.2 5.6 %patient_pass.5 = bf16[8,128,256]{2,1,0:T(8,128)(2,1)} custom-call(s32[4,128]{1,0:T(4,128)S(1)} %get-tuple-element.256.work_ref, bf16[64,128,128]{2,1,0:T(8,128)(2,1)S(1)} %get-tuple-element.257.w_ref, bf16[64,128,256]{2,1,0:T(8,128)(2,1)} %get-tuple-element.258.v_ref, bf16[8,128,256]{2,1,0:T(8,128)(2,1)S(1)} %bitcast.40), custom_call_target="tpu_custom_call" | custom-call | tf_op jit(solution)/shard_map/while/body/eval_jaxpr/patient_pass/pallas_call | solution.py:490
  170.8 3.6 %all-to-all-start.1 = ((bf16[16,64,256]{2,1,0:T(8,128)(2,1)}), bf16[16,64,256]{2,1,0:T(8,128)(2,1)S(1)}, u32[]{:S(2)}, u32[]{:S(2)}) async-start(bf16[16,64,256]{2,1,0:T(8,128)(2,1)} %bitcast.39), calls=%async_computation.1 | async-start | bytes 1048576 | tf_op jit(solution)/shard_map/while/body/eval_jaxpr/all_to_all | solution.py:447
  174.4 8.9 %all-to-all-done.1.recv_ref = bf16[16,64,256]{2,1,0:T(8,128)(2,1)S(1)} async-done(((bf16[16,64,256]{2,1,0:T(8,128)(2,1)}), bf16[16,64,256]{2,1,0:T(8,128)(2,1)S(1)}, u32[]{:S(2)}, u32[]{:S(2)}) %all-to-all-start.1) | async-done | bytes 524320 | tf_op jit(solution)/shard_map/while/body/eval_jaxpr/all_to_all | solution.py:447
  183.3 1.4 step.5
  184.7 12.6 %all_to_all.62 = bf16[16,64,256]{2,1,0:T(8,128)(2,1)S(1)} all-to-all(bf16[16,64,256]{2,1,0:T(8,128)(2,1)} %get-tuple-element.247), channel_id=1, replica_groups=mesh['rows'=8,'cols'=16] {'cols'}, dimensions={0} | all-to-all | bytes 1048576 | tf_op jit(solution)/shard_map/while/body/eval_jaxpr/all_to_all | solution.py:452
  197.3 5.6 %patient_pass.5 = bf16[8,128,256]{2,1,0:T(8,128)(2,1)} custom-call(s32[4,128]{1,0:T(4,128)S(1)} %get-tuple-element.256.work_ref, bf16[64,128,128]{2,1,0:T(8,128)(2,1)S(1)} %get-tuple-element.257.w_ref, bf16[64,128,256]{2,1,0:T(8,128)(2,1)} %get-tuple-element.258.v_ref, bf16[8,128,256]{2,1,0:T(8,128)(2,1)S(1)} %bitcast.40), custom_call_target="tpu_custom_call" | custom-call | tf_op jit(solution)/shard_map/while/body/eval_jaxpr/patient_pass/pallas_call | solution.py:490
  202.9 3.8 %all-to-all-start.1 = ((bf16[16,64,256]{2,1,0:T(8,128)(2,1)}), bf16[16,64,256]{2,1,0:T(8,128)(2,1)S(1)}, u32[]{:S(2)}, u32[]{:S(2)}) async-start(bf16[16,64,256]{2,1,0:T(8,128)(2,1)} %bitcast.39), calls=%async_computation.1 | async-start | bytes 1048576 | tf_op jit(solution)/shard_map/while/body/eval_jaxpr/all_to_all | solution.py:447
  206.7 8.9 %all-to-all-done.1.recv_ref = bf16[16,64,256]{2,1,0:T(8,128)(2,1)S(1)} async-done(((bf16[16,64,256]{2,1,0:T(8,128)(2,1)}), bf16[16,64,256]{2,1,0:T(8,128)(2,1)S(1)}, u32[]{:S(2)}, u32[]{:S(2)}) %all-to-all-start.1) | async-done | bytes 524320 | tf_op jit(solution)/shard_map/while/body/eval_jaxpr/all_to_all | solution.py:447
  215.6 1.1 step.5
  216.7 12.5 %all_to_all.61 = bf16[16,64,256]{2,1,0:T(8,128)(2,1)S(1)} all-to-all(bf16[16,64,256]{2,1,0:T(8,128)(2,1)} %get-tuple-element.167), channel_id=1, replica_groups=mesh['rows'=8,'cols'=16] {'cols'}, dimensions={0} | all-to-all | bytes 1048576 | tf_op jit(solution)/shard_map/all_to_all | solution.py:452
  229.2 0.0 collective-permute-start.5
  229.2 0.0 collective-permute-start.4
  229.2 9.2 %collective-permute-done.5.refs_6_ = bf16[8,128,256]{2,1,0:T(8,128)(2,1)S(1)} collective-permute-done((bf16[8,128,256]{2,1,0:T(8,128)(2,1)S(1)}, bf16[8,128,256]{2,1,0:T(8,128)(2,1)S(1)}, u32[]{:S(2)}, u32[]{:S(2)}) %collective-permute-start.5) | collective-permute-done | bytes 524320 | tf_op jit(solution)/shard_map/ppermute | solution.py:418
  238.4 8.9 %collective-permute-start.8 = (bf16[8,128,256]{2,1,0:T(8,128)(2,1)S(1)}, bf16[8,128,256]{2,1,0:T(8,128)(2,1)S(1)}, u32[]{:S(2)}, u32[]{:S(2)}) collective-permute-start(bf16[8,128,256]{2,1,0:T(8,128)(2,1)S(1)} %bitcast.49), channel_id=1, source_target_pairs={{0,16},{16,0},{32,48},{48,32},{64,80},{80,64},{96,112},{112,96},{1... | collective-permute-start | bytes 1572872 | tf_op jit(solution)/shard_map/ppermute | solution.py:418
  247.3 0.0 collective-permute-done.4.refs_5_
  247.3 0.1 collective-permute-start.6
  247.5 0.0 collective-permute-done.1.refs_1_
  247.5 0.1 collective-permute-start.7
  247.6 1.9 collective-permute-start.10
  249.4 0.1 collective-permute-start.9
  249.5 5.8 %collective-permute-done.6.refs_7_ = bf16[4,128,256]{2,1,0:T(8,128)(2,1)S(1)} collective-permute-done((bf16[4,128,256]{2,1,0:T(8,128)(2,1)S(1)}, bf16[4,128,256]{2,1,0:T(8,128)(2,1)S(1)}, u32[]{:S(2)}, u32[]{:S(2)}) %collective-permute-start.6) | collective-permute-done | bytes 262176 | tf_op jit(solution)/shard_map/ppermute | solution.py:418
  255.4 0.8 collective-permute-start.11
  256.1 0.6 collective-permute-done.7.refs_8_
  256.7 0.8 collective-permute-start.12
  257.5 0.0 collective-permute-done.8.refs_9_
  257.5 0.0 collective-permute-done.11.refs_12_
  257.5 1.1 collective-permute-done.12.refs_13_
  258.6 0.0 collective-permute-done.9.refs_10_
  258.7 0.6 copy-done.17
  259.4 0.2 copy-done.9
  259.5 18.1 %lab_step.1 = bf16[128,16,256]{2,1,0:T(8,128)(2,1)} custom-call(s32[1]{0:T(128)} %bitcast.3.row_ref, s32[8,128]{1,0:T(8,128)} %bitcast.61, bf16[2,2,64,16,128]{4,3,2,1,0:T(8,128)(2,1)} %get-tuple-element.163.refs_0_, bf16[2,2,64,16,128]{4,3,2,1,0:T(8,128)(2,1)} %collective-permute-done.1.refs_1_, ...), custom_call_target="tpu_custom_call" | custom-call | tf_op jit(solution)/shard_map/lab_step/pallas_call | solution.py:518
  277.7 4.0 %all-to-all-start.5 = ((bf16[8,256,256]{2,1,0:T(8,128)(2,1)}), bf16[8,256,256]{2,1,0:T(8,128)(2,1)S(1)}, u32[]{:S(2)}, u32[]{:S(2)}) async-start(bf16[8,256,256]{2,1,0:T(8,128)(2,1)} %bitcast.45), calls=%async_computation.5 | async-start | bytes 2097152 | tf_op jit(solution)/shard_map/all_to_all | solution.py:537
  281.6 1.5 slice_bitcast_fusion
  283.1 13.6 %all-to-all-done.5 = bf16[8,256,256]{2,1,0:T(8,128)(2,1)S(1)} async-done(((bf16[8,256,256]{2,1,0:T(8,128)(2,1)}), bf16[8,256,256]{2,1,0:T(8,128)(2,1)S(1)}, u32[]{:S(2)}, u32[]{:S(2)}) %all-to-all-start.5) | async-done | bytes 1048608 | tf_op jit(solution)/shard_map/all_to_all | solution.py:537
  296.8 1.7 convert_add_fusion
  (50 shorter events, 0.2 us)
Async XLA Ops:
  7.2 54.7 %copy-start = (bf16[256,256]{1,0:T(8,128)(2,1)S(1)}, bf16[256,256]{1,0:T(8,128)(2,1)}, u32[]{:S(2)}) copy-start(bf16[256,256]{1,0:T(8,128)(2,1)} %param.19) | copy-start | bytes 393220
  7.2 74.4 %all-gather.3.cloned.1.call-start = ((), (), s32[]{:S(2)}) async-start(), calls=%async_computation.6 | async-start | bytes 9437184 | tf_op jit(solution)/shard_map/all_gather | solution.py:395
  48.1 16.7 %collective-permute-start = (bf16[4,2,64,16,128]{4,3,2,1,0:T(8,128)(2,1)}, bf16[4,2,64,16,128]{4,3,2,1,0:T(8,128)(2,1)}, u32[]{:S(2)}, u32[]{:S(2)}) collective-permute-start(bf16[4,2,64,16,128]{4,3,2,1,0:T(8,128)(2,1)} %get-tuple-element.149), channel_id=1, source_target_pairs={{0,16},{16,0},{32,48},{48,32},{64,80},{80,64},{96,112},{112,96},{1... | collective-permute-start | bytes 6291464 | tf_op jit(solution)/shard_map/ppermute | solution.py:418
  64.7 2.0 copy-start.12
  64.7 2.0 copy-start.13
  66.8 1.5 copy-start.10
  66.8 1.5 copy-start.11
  88.0 25.9 %all-to-all-start.3 = ((f32[16,64,256]{2,1,0:T(8,128)}), f32[16,64,256]{2,1,0:T(8,128)S(1)}, u32[]{:S(2)}, u32[]{:S(2)}) async-start(f32[16,64,256]{2,1,0:T(8,128)} %bitcast.55), calls=%async_computation.3 | async-start | bytes 2097152 | tf_op jit(solution)/shard_map/all_to_all | solution.py:447
  96.9 150.6 %collective-permute-start.1 = (bf16[2,2,64,16,128]{4,3,2,1,0:T(8,128)(2,1)}, bf16[2,2,64,16,128]{4,3,2,1,0:T(8,128)(2,1)}, u32[]{:S(2)}, u32[]{:S(2)}) collective-permute-start(bf16[2,2,64,16,128]{4,3,2,1,0:T(8,128)(2,1)} %get-tuple-element.164), channel_id=1, source_target_pairs={{0,32},{16,48},{32,0},{48,16},{64,96},{80,112},{96,64},{112,80},{1... | collective-permute-start | bytes 3145736 | tf_op jit(solution)/shard_map/ppermute | solution.py:418
  97.0 150.6 %collective-permute-start.2 = (bf16[2,2,64,16,128]{4,3,2,1,0:T(8,128)(2,1)}, bf16[2,2,64,16,128]{4,3,2,1,0:T(8,128)(2,1)}, u32[]{:S(2)}, u32[]{:S(2)}) collective-permute-start(bf16[2,2,64,16,128]{4,3,2,1,0:T(8,128)(2,1)} %get-tuple-element.165), channel_id=1, source_target_pairs={{0,64},{16,80},{32,96},{48,112},{64,0},{80,16},{96,32},{112,48},{1... | collective-permute-start | bytes 3145736 | tf_op jit(solution)/shard_map/ppermute | solution.py:418
  97.1 152.4 %collective-permute-start.3 = (bf16[2,2,64,16,128]{4,3,2,1,0:T(8,128)(2,1)}, bf16[2,2,64,16,128]{4,3,2,1,0:T(8,128)(2,1)}, u32[]{:S(2)}, u32[]{:S(2)}) collective-permute-start(bf16[2,2,64,16,128]{4,3,2,1,0:T(8,128)(2,1)} %get-tuple-element.166), channel_id=1, source_target_pairs={{0,96},{16,112},{32,64},{48,80},{64,32},{80,48},{96,0},{112,16},{1... | collective-permute-start | bytes 3145736 | tf_op jit(solution)/shard_map/ppermute | solution.py:418
  131.4 9.2 %copy-start.3 = (f32[4,64,256]{2,1,0:T(8,128)S(1)}, f32[4,64,256]{2,1,0:T(8,128)}, u32[]{:S(2)}) copy-start(f32[4,64,256]{2,1,0:T(8,128)} %get-tuple-element.246) | copy-start | bytes 786436 | tf_op jit(solution)/shard_map/while
  131.4 19.5 %copy-start.1 = (f32[256,256]{1,0:T(8,128)S(1)}, f32[256,256]{1,0:T(8,128)}, u32[]{:S(2)}) copy-start(f32[256,256]{1,0:T(8,128)} %get-tuple-element.259.gram_ref) | copy-start | bytes 786436 | tf_op jit(solution)/shard_map/while
  137.0 13.9 %all-to-all-start.1 = ((bf16[16,64,256]{2,1,0:T(8,128)(2,1)}), bf16[16,64,256]{2,1,0:T(8,128)(2,1)S(1)}, u32[]{:S(2)}, u32[]{:S(2)}) async-start(bf16[16,64,256]{2,1,0:T(8,128)(2,1)} %bitcast.39), calls=%async_computation.1 | async-start | bytes 1048576 | tf_op jit(solution)/shard_map/while/body/eval_jaxpr/all_to_all | solution.py:447
  165.2 9.2 %copy-start.3 = (f32[4,64,256]{2,1,0:T(8,128)S(1)}, f32[4,64,256]{2,1,0:T(8,128)}, u32[]{:S(2)}) copy-start(f32[4,64,256]{2,1,0:T(8,128)} %get-tuple-element.246) | copy-start | bytes 786436 | tf_op jit(solution)/shard_map/while
  165.2 18.1 %copy-start.1 = (f32[256,256]{1,0:T(8,128)S(1)}, f32[256,256]{1,0:T(8,128)}, u32[]{:S(2)}) copy-start(f32[256,256]{1,0:T(8,128)} %get-tuple-element.259.gram_ref) | copy-start | bytes 786436 | tf_op jit(solution)/shard_map/while
  170.8 12.5 %all-to-all-start.1 = ((bf16[16,64,256]{2,1,0:T(8,128)(2,1)}), bf16[16,64,256]{2,1,0:T(8,128)(2,1)S(1)}, u32[]{:S(2)}, u32[]{:S(2)}) async-start(bf16[16,64,256]{2,1,0:T(8,128)(2,1)} %bitcast.39), calls=%async_computation.1 | async-start | bytes 1048576 | tf_op jit(solution)/shard_map/while/body/eval_jaxpr/all_to_all | solution.py:447
  197.3 9.4 %copy-start.3 = (f32[4,64,256]{2,1,0:T(8,128)S(1)}, f32[4,64,256]{2,1,0:T(8,128)}, u32[]{:S(2)}) copy-start(f32[4,64,256]{2,1,0:T(8,128)} %get-tuple-element.246) | copy-start | bytes 786436 | tf_op jit(solution)/shard_map/while
  197.3 18.3 %copy-start.1 = (f32[256,256]{1,0:T(8,128)S(1)}, f32[256,256]{1,0:T(8,128)}, u32[]{:S(2)}) copy-start(f32[256,256]{1,0:T(8,128)} %get-tuple-element.259.gram_ref) | copy-start | bytes 786436 | tf_op jit(solution)/shard_map/while
  202.9 12.7 %all-to-all-start.1 = ((bf16[16,64,256]{2,1,0:T(8,128)(2,1)}), bf16[16,64,256]{2,1,0:T(8,128)(2,1)S(1)}, u32[]{:S(2)}, u32[]{:S(2)}) async-start(bf16[16,64,256]{2,1,0:T(8,128)(2,1)} %bitcast.39), calls=%async_computation.1 | async-start | bytes 1048576 | tf_op jit(solution)/shard_map/while/body/eval_jaxpr/all_to_all | solution.py:447
  229.2 29.5 %copy-start.4 = (bf16[16,64,256]{2,1,0:T(8,128)(2,1)}, bf16[16,64,256]{2,1,0:T(8,128)(2,1)S(1)}, u32[]{:S(2)}) copy-start(bf16[16,64,256]{2,1,0:T(8,128)(2,1)S(1)} %all_to_all.61) | copy-start | bytes 1572868
  229.2 9.2 %collective-permute-start.5 = (bf16[8,128,256]{2,1,0:T(8,128)(2,1)S(1)}, bf16[8,128,256]{2,1,0:T(8,128)(2,1)S(1)}, u32[]{:S(2)}, u32[]{:S(2)}) collective-permute-start(bf16[8,128,256]{2,1,0:T(8,128)(2,1)S(1)} %bitcast.47), channel_id=1, source_target_pairs={{0,96},{16,112},{32,64},{48,80},{64,32},{80,48},{96,0},{112,16},{1... | collective-permute-start | bytes 1572872 | tf_op jit(solution)/shard_map/ppermute | solution.py:418
  229.2 18.2 %collective-permute-start.4 = (bf16[8,128,256]{2,1,0:T(8,128)(2,1)S(1)}, bf16[8,128,256]{2,1,0:T(8,128)(2,1)S(1)}, u32[]{:S(2)}, u32[]{:S(2)}) collective-permute-start(bf16[8,128,256]{2,1,0:T(8,128)(2,1)S(1)} %bitcast.48), channel_id=1, source_target_pairs={{0,32},{16,48},{32,0},{48,16},{64,96},{80,112},{96,64},{112,80},{1... | collective-permute-start | bytes 1572872 | tf_op jit(solution)/shard_map/ppermute | solution.py:418
  238.4 20.3 %copy-start.5 = (bf16[8,128,256]{2,1,0:T(8,128)(2,1)}, bf16[8,128,256]{2,1,0:T(8,128)(2,1)S(1)}, u32[]{:S(2)}) copy-start(bf16[8,128,256]{2,1,0:T(8,128)(2,1)S(1)} %collective-permute-done.5.refs_6_) | copy-start | bytes 1572868
  238.4 19.1 %collective-permute-start.8 = (bf16[8,128,256]{2,1,0:T(8,128)(2,1)S(1)}, bf16[8,128,256]{2,1,0:T(8,128)(2,1)S(1)}, u32[]{:S(2)}, u32[]{:S(2)}) collective-permute-start(bf16[8,128,256]{2,1,0:T(8,128)(2,1)S(1)} %bitcast.49), channel_id=1, source_target_pairs={{0,16},{16,0},{32,48},{48,32},{64,80},{80,64},{96,112},{112,96},{1... | collective-permute-start | bytes 1572872 | tf_op jit(solution)/shard_map/ppermute | solution.py:418
  247.3 11.3 %copy-start.6 = (bf16[8,128,256]{2,1,0:T(8,128)(2,1)}, bf16[8,128,256]{2,1,0:T(8,128)(2,1)S(1)}, u32[]{:S(2)}) copy-start(bf16[8,128,256]{2,1,0:T(8,128)(2,1)S(1)} %collective-permute-done.4.refs_5_) | copy-start | bytes 1572868
  247.3 8.0 %collective-permute-start.6 = (bf16[4,128,256]{2,1,0:T(8,128)(2,1)S(1)}, bf16[4,128,256]{2,1,0:T(8,128)(2,1)S(1)}, u32[]{:S(2)}, u32[]{:S(2)}) collective-permute-start(bf16[4,128,256]{2,1,0:T(8,128)(2,1)S(1)} %slice.32), channel_id=1, source_target_pairs={{0,32},{16,48},{32,0},{48,16},{64,96},{80,112},{96,64},{112,80},{1... | collective-permute-start | bytes 786440 | tf_op jit(solution)/shard_map/ppermute | solution.py:418
  247.5 9.2 %collective-permute-start.7 = (bf16[4,128,256]{2,1,0:T(8,128)(2,1)S(1)}, bf16[4,128,256]{2,1,0:T(8,128)(2,1)S(1)}, u32[]{:S(2)}, u32[]{:S(2)}) collective-permute-start(bf16[4,128,256]{2,1,0:T(8,128)(2,1)S(1)} %slice.33), channel_id=1, source_target_pairs={{0,96},{16,112},{32,64},{48,80},{64,32},{80,48},{96,0},{112,16},{1... | collective-permute-start | bytes 786440 | tf_op jit(solution)/shard_map/ppermute | solution.py:418
  247.6 9.9 %collective-permute-start.10 = (bf16[8,128,256]{2,1,0:T(8,128)(2,1)S(1)}, bf16[8,128,256]{2,1,0:T(8,128)(2,1)S(1)}, u32[]{:S(2)}, u32[]{:S(2)}) collective-permute-start(bf16[8,128,256]{2,1,0:T(8,128)(2,1)S(1)} %collective-permute-done.5.refs_6_), channel_id=1, source_target_pairs={{0,16},{16,0},{32,48},{48,32},{64,80},{80,64},{96,112},{112,96},{1... | collective-permute-start | bytes 1572872 | tf_op jit(solution)/shard_map/ppermute | solution.py:418
  249.4 9.2 %collective-permute-start.9 = (bf16[8,128,256]{2,1,0:T(8,128)(2,1)S(1)}, bf16[8,128,256]{2,1,0:T(8,128)(2,1)S(1)}, u32[]{:S(2)}, u32[]{:S(2)}) collective-permute-start(bf16[8,128,256]{2,1,0:T(8,128)(2,1)S(1)} %collective-permute-done.4.refs_5_), channel_id=1, source_target_pairs={{0,16},{16,0},{32,48},{48,32},{64,80},{80,64},{96,112},{112,96},{1... | collective-permute-start | bytes 1572872 | tf_op jit(solution)/shard_map/ppermute | solution.py:418
  255.4 3.3 %copy-start.14 = (bf16[4,128,256]{2,1,0:T(8,128)(2,1)}, bf16[4,128,256]{2,1,0:T(8,128)(2,1)S(1)}, u32[]{:S(2)}) copy-start(bf16[4,128,256]{2,1,0:T(8,128)(2,1)S(1)} %collective-permute-done.6.refs_7_) | copy-start | bytes 786436
  255.4 2.1 collective-permute-start.11
  256.7 2.0 copy-start.15
  256.7 1.9 collective-permute-start.12
  257.5 1.2 copy-start.7
  257.5 1.2 copy-start.16
  257.5 1.2 copy-start.8
  258.6 0.7 copy-start.17
  258.6 0.9 copy-start.9
  277.7 19.1 %copy-start.2 = (bf16[16,128,256]{2,1,0:T(8,128)(2,1)S(1)}, bf16[16,128,256]{2,1,0:T(8,128)(2,1)}, u32[]{:S(2)}) copy-start(bf16[16,128,256]{2,1,0:T(8,128)(2,1)} %all_to_all.60) | copy-start | bytes 3145732
  277.7 19.1 %all-to-all-start.5 = ((bf16[8,256,256]{2,1,0:T(8,128)(2,1)}), bf16[8,256,256]{2,1,0:T(8,128)(2,1)S(1)}, u32[]{:S(2)}, u32[]{:S(2)}) async-start(bf16[8,256,256]{2,1,0:T(8,128)(2,1)} %bitcast.45), calls=%async_computation.5 | async-start | bytes 2097152 | tf_op jit(solution)/shard_map/all_to_all | solution.py:537
Sparse Core Ops, SparseCore 0:
  31.8 49.7 all-gather.2
